TPU v7x, 32 devices: a whole 2x2x4 slice. The times are simulated.
32 devices in a mesh: aux: 4 (over x, core), basis: 8 (over z, y).
Axes of the slice: x: 2, y: 2, z: 4, core: 2. Of those that a mesh axis runs over, the one named last changes fastest.
Arguments:
- v_blocks: bfloat16 [32, 384, 128, 128], P('aux', 'basis'), may hold values from -6 to 6
- pair_map: int32 [4, 384, 2], P('aux', 'basis'), may hold values from 0 to 239, as said below
- pair_count: int32 [4, 8], P('aux', 'basis'), may hold values from 2 to 48, as said below
- occ_coef: bfloat16 [8, 30720], P(None, 'basis'), may hold values from -0.375 to 0.375
- virt_coef: bfloat16 [30720, 32768], P('basis', 'aux'), may hold values from -0.03125 to 0.03125
Outputs:
- b_tensor: bfloat16 [32768, 256], P(('aux', 'basis'))
Inputs may be any that keep to these rules, and one draw needn't show every extreme that they name: pair_map[s, k, 0] lies in the blocks of basis index k // 48 (blocks b * 240 / 8 onward); pair_map[s, k, 1] lies within 8 blocks of it, cyclically over 240 blocks, and that distance 8 is reached. Only the first pair_count slots of a device are live; in every slab some basis index has all 48 live.
All inputs are finite; a program needn't handle non-finite values.
Results may differ from a plain program's by a relative error of at most 0.0049.
Values may be sent and summed in bfloat16 or wider, within the bound.
No kernel may reach another device: no remote copies, remote signals or barrier semaphores. Data moves between devices by JAX's collectives and lax.ppermute only.
A program may use at most 192 MiB of HBM per device.

v0:
```python
import functools

import jax
import jax.numpy as jnp
from jax import lax
from jax.experimental import pallas as pl
from jax.experimental.pallas import tpu as pltpu
from jax.sharding import PartitionSpec as P

BB = 128
NEAR = 8
SECOND, THIRD = -1, -2
F32 = jnp.float32
BF16 = jnp.bfloat16
VMEM = pl.BlockSpec(memory_space=pltpu.VMEM)
SMEM = pl.BlockSpec(memory_space=pltpu.SMEM)
HBM = pl.BlockSpec(memory_space=pltpu.HBM)
ANY = pl.BlockSpec(memory_space=pl.ANY)


def exchange(array, axis, bit):
    peers = lax.axis_size(axis)
    return lax.ppermute(array, axis, [(i, i ^ bit) for i in range(peers)])


def divisor(length, most):
    return max(d for d in range(1, most + 1) if length % d == 0)


def chunk_columns(basis, step, kept, width):
    if step in (SECOND, THIRD):
        inside = ((basis >> 1) ^ (basis >> 2)) & 1
        step = 2 - inside if step == SECOND else 1 + inside
    chunk = basis ^ (2 * step + (0 if kept else 1))
    return pl.ds(pl.multiple_of(chunk * width, BB), width)


def half_kernel(
    groups, blocks, following, basis_ref, map_ref, count_ref, table_ref, pair_ref, next_ref, v_ref, virt_ref,
    out_ref, carry_ref, buf_ref, acc_ref, occ_ref, sems,
):
    q = v_ref.shape[0]
    nocc, halo = pair_ref.shape
    here = table_ref.shape[1] - 2 * halo
    per = v_ref.shape[1] // groups
    blocks_here = here // BB
    first = basis_ref[0] * blocks_here
    copies = [
        pltpu.make_async_copy(v_ref.at[:, pl.ds(g * per, per)], buf_ref.at[g], sems.at[g]) for g in range(groups)
    ]
    columns = chunk_columns(basis_ref[0], *following, carry_ref.shape[1])
    carry = pltpu.make_async_copy(virt_ref.at[pl.ds(0, carry_ref.shape[0]), columns], carry_ref, sems.at[groups])
    for copy in (*copies, carry):
        copy.start()

    acc_ref[...] = jnp.zeros_like(acc_ref)
    odd = basis_ref[0] % 2
    occ_ref[...] = table_ref[...]
    occ_ref[:, pl.ds(pl.multiple_of((1 - odd) * (halo + here), BB), halo)] = pair_ref[...]
    occ_ref[:, pl.ds(pl.multiple_of(odd * (halo + here), BB), halo)] = next_ref[...]

    def picked(k):
        source = lax.rem(map_ref[0, k, 1] - first + NEAR + blocks, blocks)
        rows = occ_ref[:, pl.ds(pl.multiple_of(source * BB, BB), BB)]
        return jnp.where(k < count_ref[0, 0], rows, jnp.zeros_like(rows))

    for g in range(groups):
        copies[g].wait()
        sums = []
        for j in range(0, per, 2):
            k = g * per + j
            if j + 1 < per:
                one, two = picked(k), picked(k + 1)
                none = jnp.zeros_like(one)
                left = jnp.concatenate(
                    [jnp.concatenate([one, none], axis=1), jnp.concatenate([none, two], axis=1)], axis=0
                )
                right = jnp.concatenate([buf_ref[g, :, j], buf_ref[g, :, j + 1]], axis=-1).reshape(q * BB, 2 * BB)
            else:
                left, right = picked(k), buf_ref[g, :, j].reshape(q * BB, BB)
            sums.append(lax.dot_general(left, right, (((1,), (1,)), ((), ())), preferred_element_type=F32))
        for j in range(per):
            rows = sums[j // 2][(j % 2) * nocc : (j % 2 + 1) * nocc]
            target = pl.multiple_of((map_ref[0, g * per + j, 0] - first) * BB, BB)
            for p in range(q):
                acc_ref[p * nocc : (p + 1) * nocc, pl.ds(target, BB)] += rows[:, p * BB : (p + 1) * BB]
    out_ref[...] = acc_ref[...].astype(BF16)
    carry.wait()


def half_rows(basis, pair_map, pair_count, table, pair, after, v_blocks, virt, blocks, width, following):
    q, pairs = v_blocks.shape[:2]
    nocc, halo = pair.shape
    here = table.shape[1] - 2 * halo
    groups = pairs // divisor(pairs, 4)
    return pl.pallas_call(
        functools.partial(half_kernel, groups, blocks, following),
        in_specs=[SMEM, SMEM, SMEM, VMEM, VMEM, VMEM, HBM, HBM],
        out_specs=[VMEM, VMEM],
        scratch_shapes=[
            pltpu.VMEM((groups, q, pairs // groups, BB, BB), BF16),
            pltpu.VMEM((q * nocc, here), F32),
            pltpu.VMEM((nocc, here + 2 * halo), BF16),
            pltpu.SemaphoreType.DMA((groups + 1,)),
        ],
        out_shape=[
            jax.ShapeDtypeStruct((q * nocc, here), BF16),
            jax.ShapeDtypeStruct((carried(virt.shape[0]), width), BF16),
        ],
        compiler_params=pltpu.CompilerParams(vmem_limit_bytes=50 * 2**20),
        cost_estimate=pl.CostEstimate(
            flops=2 * v_blocks.size * nocc, bytes_accessed=2 * v_blocks.size, transcendentals=0
        ),
    )(basis, pair_map, pair_count, table, pair, after, v_blocks, virt)


def carried(depth):
    return min(768, depth // 2)


def cuts_of(depth):
    start = carried(depth)
    return [(at, min(768, depth - at)) for at in range(start, depth, 768)]


def joined(refs):
    return jnp.concatenate([ref[...] for ref in refs], axis=0).astype(F32)


def product_kernel(step, kept, following, parts, adds, basis_ref, virt_ref, first_ref, *refs):
    half_refs, refs = refs[:parts], refs[parts:]
    add_refs = refs[: sum(adds)]
    out_ref, *carry_refs, buf_ref, acc_ref, sems = refs[-5 if following else -4 :]
    width = acc_ref.shape[1]
    columns = chunk_columns(basis_ref[0], step, kept, width)
    cuts = cuts_of(virt_ref.shape[0])
    copies = [
        pltpu.make_async_copy(
            virt_ref.at[pl.ds(start, size), columns], buf_ref.at[pl.ds(start - cuts[0][0], size)], sems.at[i]
        )
        for i, (start, size) in enumerate(cuts)
    ]
    for carry_ref in carry_refs:
        after = chunk_columns(basis_ref[0], *following, width)
        copies.append(
            pltpu.make_async_copy(
                virt_ref.at[pl.ds(0, carry_ref.shape[0]), after], carry_ref, sems.at[len(cuts)]
            )
        )
    for copy in copies:
        copy.start()

    def term(start, block):
        rows = jnp.concatenate([ref[:, start : start + block.shape[0]] for ref in half_refs], axis=0)
        return jnp.dot(rows, block, preferred_element_type=F32)

    total = term(0, first_ref[...])
    at = 0
    for count in adds:
        total += joined(add_refs[at : at + count])
        at += count
    acc_ref[...] = total
    for i, (start, size) in enumerate(cuts):
        copies[i].wait()
        total = acc_ref[...] + term(start, buf_ref[start - cuts[0][0] : start - cuts[0][0] + size])
        if i < len(cuts) - 1:
            acc_ref[...] = total
        else:
            out_ref[...] = total.astype(out_ref.dtype)
    for copy in copies[len(cuts) :]:
        copy.wait()


def product(basis, virt, first, step, kept, following, parts, adds=(), after=(), dtype=BF16):
    rows = sum(part.shape[0] for part in parts)
    depth, width = virt.shape[0], first.shape[1]
    flat = [block for add in adds for block in add]
    shapes = [jax.ShapeDtypeStruct((rows, width), dtype)]
    if following:
        shapes.append(jax.ShapeDtypeStruct(first.shape, BF16))
    return pl.pallas_call(
        functools.partial(product_kernel, step, kept, following, len(parts), tuple(len(add) for add in adds)),
        in_specs=[SMEM, HBM] + [VMEM] * (1 + len(parts) + len(flat)) + [ANY] * len(after),
        out_specs=[VMEM] * len(shapes),
        scratch_shapes=[
            pltpu.VMEM((depth - first.shape[0], width), BF16),
            pltpu.VMEM((rows, width), F32),
            pltpu.SemaphoreType.DMA((len(cuts_of(depth)) + 1,)),
        ],
        out_shape=shapes,
        compiler_params=pltpu.CompilerParams(vmem_limit_bytes=16 * 2**20),
        cost_estimate=pl.CostEstimate(
            flops=2 * rows * depth * width, bytes_accessed=2 * depth * width, transcendentals=0
        ),
    )(basis, virt, first, *parts, *flat, *after)


def finish_kernel(slab, adds, aux_ref, total_ref, *refs):
    add_refs, (out_ref, acc_ref) = refs[: sum(adds)], refs[-2:]
    total = total_ref[...]
    at = 0
    for count in adds:
        total += joined(add_refs[at : at + count])
        at += count
    acc_ref[...] = total
    for s in range(acc_ref.shape[0] // slab):
        rows = acc_ref[pl.ds(pl.multiple_of((aux_ref[0] ^ s) * slab, slab), slab), :]
        out_ref[:, s * slab : (s + 1) * slab] = rows.T.astype(BF16)


def finish(aux, total, adds, slab):
    flat = [block for add in adds for block in add]
    return pl.pallas_call(
        functools.partial(finish_kernel, slab, tuple(len(add) for add in adds)),
        in_specs=[SMEM] + [VMEM] * (1 + len(flat)),
        out_specs=VMEM,
        scratch_shapes=[pltpu.VMEM(total.shape, F32)],
        out_shape=jax.ShapeDtypeStruct(total.shape[::-1], BF16),
        compiler_params=pltpu.CompilerParams(vmem_limit_bytes=16 * 2**20),
    )(aux, total, *flat)


def local(v_blocks, pair_map, pair_count, occ_coef, virt_coef):
    peers = lax.axis_size("basis")
    slabs = lax.axis_size("aux")
    aux = lax.axis_index("aux").astype(jnp.int32)
    basis = lax.axis_index("basis").astype(jnp.int32)
    blocks = virt_coef.shape[0] // BB * peers
    halo = NEAR * BB

    even = basis % 2 == 0
    first, last = occ_coef[:, :halo], occ_coef[:, -halo:]
    pair = exchange(jnp.where(even, last, first), "basis", 1)
    ring = [(i, (i + 1 if i % 2 else i - 1) % peers) for i in range(peers)]
    after = lax.ppermute(jnp.where(even, first, last), "basis", ring)
    table = jnp.pad(occ_coef, ((0, 0), (halo, halo)))
    width = virt_coef.shape[1] // peers
    groups = peers // 2
    top, second, *others = range(groups - 1, -1, -1)
    if groups == 4:
        second, others = SECOND, [THIRD, 0]
    sends = [(m, False) for m in (top, second)]
    keeps = [(m, True) for m in (top, second, *others)]
    if groups == 4:
        order = [*sends, *sends, (THIRD, False), *keeps[:2], keeps[3], keeps[2], (0, False)]
    else:
        order = [*sends, *sends, *((m, False) for m in others), *keeps]
    number = basis.reshape(1)
    own, first = half_rows(
        number, pair_map, pair_count, table, pair, after, v_blocks, virt_coef, blocks, width, order[0]
    )
    carry = [first]

    def mult(step, kept, parts, adds=(), after=(), dtype=BF16):
        assert order.pop(0) == (step, kept)
        following = order[0] if order else None
        out, *carry[:] = product(number, virt_coef, carry[0], step, kept, following, parts, adds, after, dtype)
        return out

    def send(step, parts, after=()):
        return exchange(mult(step, False, parts, after=after), "basis", 1)

    early = [own, exchange(own, "aux", 1)]
    far = [own]
    bit = slabs // 2
    while bit > 1:
        far += [exchange(rows, "aux", bit) for rows in far]
        bit //= 2
    far = far[1:]
    received = {top: (send(top, early),)}
    received[second] = (send(second, early),)
    *far, _, _ = lax.optimization_barrier((*far, carry[0], received[top][0]))
    late = [block for rows in far for block in (rows, exchange(rows, "aux", 1))]
    every = early + late
    received[top] += (send(top, late),)
    received[second] += (send(second, late),)
    if groups == 4:
        received[THIRD] = (send(THIRD, every, received[SECOND][:1]),)
        sent = mult(3, True, every, (received[3],))
        along = lambda pairs: [(2 * a + s, 2 * b + s) for a, b in pairs for s in (0, 1)]
        relayed = lax.ppermute(sent, "basis", along([(0, 1), (3, 2)]))
        inner = lax.ppermute(sent, "basis", along([(1, 2), (2, 1)]))
        sent = mult(SECOND, True, every, (received[SECOND],))
        third = lax.ppermute(sent, "basis", along([(0, 2), (3, 1), (1, 0), (2, 3)]))
        total = mult(0, True, every, dtype=F32)
        part = mult(THIRD, True, every, (received[THIRD],), dtype=F32)
        sent = (part + relayed.astype(F32)).astype(BF16)
        fourth = lax.ppermute(sent, "basis", along([(1, 3), (2, 0), (0, 1), (3, 2)]))
        received[0] = (send(0, every, after=(sent, inner)),)
        third, fourth = lax.optimization_barrier((third, fourth))
        adds = (received[0], (inner,), (third,), (fourth,))
    else:
        for m in others:
            received[m] = (send(m, every),)
        adds = (received[0],)
        for m in (top, second, *others[:-1]):
            sent = mult(m, True, every, (received[m],))
            adds += ((exchange(sent, "basis", 2 * m),),)
        total = mult(0, True, every, dtype=F32)
    return finish(aux.reshape(1), total, adds, own.shape[0])


def solution(mesh):
    in_specs = (
        P("aux", "basis", None, None),
        P("aux", "basis", None),
        P("aux", "basis"),
        P(None, "basis"),
        P("basis", "aux"),
    )
    out_specs = P(("aux", "basis"), None)
    return jax.shard_map(local, mesh=mesh, in_specs=in_specs, out_specs=out_specs, check_vma=False)
```

profile of v0, /device:TPU:0, one launch (start us, length us, event | category | flops | bytes accessed | tf_op | source)
XLA Modules:
  0.0 91.6 jit_solution(8454091854798825143)
XLA Ops:
  0.0 0.7 broadcast_select_fusion
  0.7 3.0 %collective-permute-start = (bf16[8,1024]{1,0:T(8,128)(2,1)S(1)}, bf16[8,1024]{1,0:T(8,128)(2,1)S(1)}, u32[]{:S(2)}, u32[]{:S(2)}) collective-permute-start(bf16[8,1024]{1,0:T(8,128)(2,1)S(1)} %get-tuple-element.52), channel_id=1, source_target_pairs={{0,1},{1,0},{2,3},{3,2},{4,5},{5,4},{6,7},{7,6},{8,9},{9,8},{10,11... | collective-permute-start | bytes 49160 | tf_op jit(solution)/shard_map/ppermute | solution.py:23
  3.7 3.5 %collective-permute-start.1 = (bf16[8,1024]{1,0:T(8,128)(2,1)S(1)}, bf16[8,1024]{1,0:T(8,128)(2,1)S(1)}, u32[]{:S(2)}, u32[]{:S(2)}) collective-permute-start(bf16[8,1024]{1,0:T(8,128)(2,1)S(1)} %get-tuple-element.51), channel_id=1, source_target_pairs={{0,7},{1,2},{2,1},{3,4},{4,3},{5,6},{6,5},{7,0},{8,15},{9,10},{10,... | collective-permute-start | bytes 49160 | tf_op jit(solution)/shard_map/ppermute | solution.py:235
  7.3 0.8 copy.6.map_ref
  8.7 0.8 pad.4.table_ref
  9.5 0.0 collective-permute-done.pair_ref
  9.5 0.6 collective-permute-done.1.next_ref
  10.1 7.0 %shard_map.55 = (bf16[64,3840]{1,0:T(8,128)(2,1)S(1)}, bf16[768,1024]{1,0:T(8,128)(2,1)S(1)}) custom-call(s32[1]{0:T(128)} %bitcast.1.basis_ref, s32[1,48,2]{2,1,0:T(8,128)S(1)} %copy.6.map_ref, s32[1,1]{1,0:T(1,128)S(6)} %copy.7.count_ref, bf16[8,5888]{1,0:T(8,128)(2,1)S(1)} %pad.4.table_ref, bf16[8,1024]{1,0:T(8,128)(2,1)S(1)} %collective-permute-done.pair_ref, ...), custom_call_target="tpu_custom_call" | custom-call | flops 100663296 | bytes 12582912 | tf_op jit(solution)/shard_map/pallas_call | solution.py:96
  17.2 0.1 collective-permute-start.2
  17.3 1.6 %collective-permute-start.3 = (bf16[64,3840]{1,0:T(8,128)(2,1)S(1)}, bf16[64,3840]{1,0:T(8,128)(2,1)S(1)}, u32[]{:S(2)}, u32[]{:S(2)}) collective-permute-start(bf16[64,3840]{1,0:T(8,128)(2,1)S(1)} %get-tuple-element.29.refs_0_), channel_id=1, source_target_pairs={{0,16},{8,24},{16,0},{24,8},{1,17},{9,25},{17,1},{25,9},{2,18},{10... | collective-permute-start | bytes 1474568 | tf_op jit(solution)/shard_map/ppermute | solution.py:23
  18.8 0.3 collective-permute-done.2.refs_1_
  19.1 3.4 %shard_map.56 = (bf16[128,1024]{1,0:T(8,128)(2,1)S(1)}, bf16[768,1024]{1,0:T(8,128)(2,1)S(1)}) custom-call(s32[1]{0:T(128)} %bitcast.1.basis_ref, bf16[3840,8192]{1,0:T(8,128)(2,1)} %virt_ref.21, bf16[768,1024]{1,0:T(8,128)(2,1)S(1)} %get-tuple-element.28.first_ref, bf16[64,3840]{1,0:T(8,128)(2,1)S(1)} %get-tuple-element.29.refs_0_, ...), custom_call_target="tpu_custom_call" | custom-call | flops 1006632960 | bytes 7864320 | tf_op jit(solution)/shard_map/pallas_call | solution.py:181
  22.5 0.1 collective-permute-start.4
  22.6 3.4 %shard_map.57 = (bf16[128,1024]{1,0:T(8,128)(2,1)S(1)}, bf16[768,1024]{1,0:T(8,128)(2,1)S(1)}) custom-call(s32[1]{0:T(128)} %bitcast.1.basis_ref, bf16[3840,8192]{1,0:T(8,128)(2,1)} %virt_ref.21, bf16[768,1024]{1,0:T(8,128)(2,1)S(1)} %get-tuple-element.30.first_ref, bf16[64,3840]{1,0:T(8,128)(2,1)S(1)} %get-tuple-element.29.refs_0_, ...), custom_call_target="tpu_custom_call" | custom-call | flops 1006632960 | bytes 7864320 | tf_op jit(solution)/shard_map/pallas_call | solution.py:181
  26.0 4.9 %collective-permute-done.3.refs_0_.refs_2_ = bf16[64,3840]{1,0:T(8,128)(2,1)S(1)} collective-permute-done((bf16[64,3840]{1,0:T(8,128)(2,1)S(1)}, bf16[64,3840]{1,0:T(8,128)(2,1)S(1)}, u32[]{:S(2)}, u32[]{:S(2)}) %collective-permute-start.3) | collective-permute-done | bytes 491552 | tf_op jit(solution)/shard_map/ppermute | solution.py:23
  30.9 0.0 collective-permute-done.4.refs_4_
  30.9 0.0 collective-permute-start.5
  30.9 0.3 collective-permute-start.6
  31.2 1.6 %collective-permute-done.5.refs_1_.refs_3_ = bf16[64,3840]{1,0:T(8,128)(2,1)S(1)} collective-permute-done((bf16[64,3840]{1,0:T(8,128)(2,1)S(1)}, bf16[64,3840]{1,0:T(8,128)(2,1)S(1)}, u32[]{:S(2)}, u32[]{:S(2)}) %collective-permute-start.5) | collective-permute-done | bytes 491552 | tf_op jit(solution)/shard_map/ppermute | solution.py:23
  32.8 3.4 %shard_map.58 = (bf16[128,1024]{1,0:T(8,128)(2,1)S(1)}, bf16[768,1024]{1,0:T(8,128)(2,1)S(1)}) custom-call(s32[1]{0:T(128)} %bitcast.1.basis_ref, bf16[3840,8192]{1,0:T(8,128)(2,1)} %virt_ref.21, bf16[768,1024]{1,0:T(8,128)(2,1)S(1)} %get-tuple-element.31.first_ref, bf16[64,3840]{1,0:T(8,128)(2,1)S(1)} %collective-permute-done.3.refs_0_.refs_2_, ...), custom_call_target="tpu_custom_call" | custom-call | flops 1006632960 | bytes 7864320 | tf_op jit(solution)/shard_map/pallas_call | solution.py:181
  36.2 0.4 collective-permute-start.7
  36.6 3.4 %shard_map.59 = (bf16[128,1024]{1,0:T(8,128)(2,1)S(1)}, bf16[768,1024]{1,0:T(8,128)(2,1)S(1)}) custom-call(s32[1]{0:T(128)} %bitcast.1.basis_ref, bf16[3840,8192]{1,0:T(8,128)(2,1)} %virt_ref.21, bf16[768,1024]{1,0:T(8,128)(2,1)S(1)} %get-tuple-element.34.first_ref, bf16[64,3840]{1,0:T(8,128)(2,1)S(1)} %collective-permute-done.3.refs_0_.refs_2_, ...), custom_call_target="tpu_custom_call" | custom-call | flops 1006632960 | bytes 7864320 | tf_op jit(solution)/shard_map/pallas_call | solution.py:181
  40.0 1.8 %collective-permute-start.8 = (bf16[128,1024]{1,0:T(8,128)(2,1)S(1)}, bf16[128,1024]{1,0:T(8,128)(2,1)S(1)}, u32[]{:S(2)}, u32[]{:S(2)}) collective-permute-start(bf16[128,1024]{1,0:T(8,128)(2,1)S(1)} %get-tuple-element.40), channel_id=1, source_target_pairs={{0,1},{1,0},{2,3},{3,2},{4,5},{5,4},{6,7},{7,6},{8,9},{9,8},{10,11... | collective-permute-start | bytes 786440 | tf_op jit(solution)/shard_map/ppermute | solution.py:23
  41.8 0.0 collective-permute-done.6.refs_4_
  41.8 3.8 %shard_map.60 = (bf16[256,1024]{1,0:T(8,128)(2,1)S(1)}, bf16[768,1024]{1,0:T(8,128)(2,1)S(1)}) custom-call(s32[1]{0:T(128)} %bitcast.1.basis_ref, bf16[3840,8192]{1,0:T(8,128)(2,1)} %virt_ref.21, bf16[768,1024]{1,0:T(8,128)(2,1)S(1)} %get-tuple-element.35.first_ref, bf16[64,3840]{1,0:T(8,128)(2,1)S(1)} %get-tuple-element.29.refs_0_, ...), custom_call_target="tpu_custom_call" | custom-call | flops 2013265920 | bytes 7864320 | tf_op jit(solution)/shard_map/pallas_call | solution.py:181
  45.6 0.3 collective-permute-start.9
  45.9 0.0 collective-permute-done.7.refs_5_
  45.9 3.5 %shard_map.61 = (bf16[256,1024]{1,0:T(8,128)(2,1)S(1)}, bf16[768,1024]{1,0:T(8,128)(2,1)S(1)}) custom-call(s32[1]{0:T(128)} %bitcast.1.basis_ref, bf16[3840,8192]{1,0:T(8,128)(2,1)} %virt_ref.21, bf16[768,1024]{1,0:T(8,128)(2,1)S(1)} %get-tuple-element.37.first_ref, bf16[64,3840]{1,0:T(8,128)(2,1)S(1)} %get-tuple-element.29.refs_0_, ...), custom_call_target="tpu_custom_call" | custom-call | flops 2013265920 | bytes 7864320 | tf_op jit(solution)/shard_map/pallas_call | solution.py:181
  49.5 2.1 %collective-permute-start.10 = (bf16[256,1024]{1,0:T(8,128)(2,1)S(1)}, bf16[256,1024]{1,0:T(8,128)(2,1)S(1)}, u32[]{:S(2)}, u32[]{:S(2)}) collective-permute-start(bf16[256,1024]{1,0:T(8,128)(2,1)S(1)} %get-tuple-element.47), channel_id=1, source_target_pairs={{0,2},{1,3},{6,4},{7,5},{8,10},{9,11},{14,12},{15,13},{16,18},{17,... | collective-permute-start | bytes 1572872 | tf_op jit(solution)/shard_map/ppermute | solution.py:281
  51.6 0.9 collective-permute-start.11
  52.5 0.0 collective-permute-done.8.refs_5_
  52.5 4.4 %shard_map.62 = (bf16[256,1024]{1,0:T(8,128)(2,1)}, bf16[768,1024]{1,0:T(8,128)(2,1)S(1)}) custom-call(s32[1]{0:T(128)} %bitcast.1.basis_ref, bf16[3840,8192]{1,0:T(8,128)(2,1)} %virt_ref.21, bf16[768,1024]{1,0:T(8,128)(2,1)S(1)} %get-tuple-element.39.first_ref, bf16[64,3840]{1,0:T(8,128)(2,1)S(1)} %get-tuple-element.29.refs_0_, ...), custom_call_target="tpu_custom_call" | custom-call | flops 2013265920 | bytes 7864320 | tf_op jit(solution)/shard_map/pallas_call | solution.py:181
  56.9 2.1 %collective-permute-start.13 = (bf16[256,1024]{1,0:T(8,128)(2,1)}, bf16[256,1024]{1,0:T(8,128)(2,1)S(1)}, u32[]{:S(2)}, u32[]{:S(2)}) collective-permute-start(bf16[256,1024]{1,0:T(8,128)(2,1)} %get-tuple-element.48), channel_id=1, source_target_pairs={{0,4},{1,5},{6,2},{7,3},{2,0},{3,1},{4,6},{5,7},{8,12},{9,13},{14,... | collective-permute-start | bytes 1572872 | tf_op jit(solution)/shard_map/ppermute | solution.py:284
  59.0 3.8 %shard_map.63 = (f32[256,1024]{1,0:T(8,128)S(1)}, bf16[768,1024]{1,0:T(8,128)(2,1)S(1)}) custom-call(s32[1]{0:T(128)} %bitcast.1.basis_ref, bf16[3840,8192]{1,0:T(8,128)(2,1)} %virt_ref.21, bf16[768,1024]{1,0:T(8,128)(2,1)S(1)} %get-tuple-element.41.first_ref, bf16[64,3840]{1,0:T(8,128)(2,1)S(1)} %get-tuple-element.29.refs_0_, ...), custom_call_target="tpu_custom_call" | custom-call | flops 2013265920 | bytes 7864320 | tf_op jit(solution)/shard_map/pallas_call | solution.py:181
  62.8 0.0 collective-permute-done.9.refs_4_
  62.8 3.8 %shard_map.64 = (f32[256,1024]{1,0:T(8,128)S(1)}, bf16[768,1024]{1,0:T(8,128)(2,1)S(1)}) custom-call(s32[1]{0:T(128)} %bitcast.1.basis_ref, bf16[3840,8192]{1,0:T(8,128)(2,1)} %virt_ref.21, bf16[768,1024]{1,0:T(8,128)(2,1)S(1)} %get-tuple-element.43.first_ref, bf16[64,3840]{1,0:T(8,128)(2,1)S(1)} %get-tuple-element.29.refs_0_, ...), custom_call_target="tpu_custom_call" | custom-call | flops 2013265920 | bytes 7864320 | tf_op jit(solution)/shard_map/pallas_call | solution.py:181
  66.7 0.0 collective-permute-done.10
  66.7 0.2 add_convert_fusion.refs_4_
  66.8 0.2 collective-permute-start.14
  67.0 0.0 collective-permute-done.11.refs_5_.refs_1_
  67.0 3.6 %shard_map.65 = bf16[256,1024]{1,0:T(8,128)(2,1)S(1)} custom-call(s32[1]{0:T(128)} %bitcast.1.basis_ref, bf16[3840,8192]{1,0:T(8,128)(2,1)} %virt_ref.21, bf16[768,1024]{1,0:T(8,128)(2,1)S(1)} %get-tuple-element.45.first_ref, bf16[64,3840]{1,0:T(8,128)(2,1)S(1)} %get-tuple-element.29.refs_0_, bf16[64,3840]{1,0:T(8,128)(2,1)S(1)} %collective-permute-done.2.refs_1_, ...), custom_call_target="tpu_custom_call" | custom-call | flops 2013265920 | bytes 7864320 | tf_op jit(solution)/shard_map/pallas_call | solution.py:181
  70.6 1.4 %collective-permute-start.12 = (bf16[256,1024]{1,0:T(8,128)(2,1)S(1)}, bf16[256,1024]{1,0:T(8,128)(2,1)}, u32[]{:S(2)}, u32[]{:S(2)}) collective-permute-start(bf16[256,1024]{1,0:T(8,128)(2,1)S(1)} %shard_map.65), channel_id=1, source_target_pairs={{0,1},{1,0},{2,3},{3,2},{4,5},{5,4},{6,7},{7,6},{8,9},{9,8},{10,11... | collective-permute-start | bytes 1572872 | tf_op jit(solution)/shard_map/ppermute | solution.py:23
  72.0 3.3 %collective-permute-done.13.refs_2_ = bf16[256,1024]{1,0:T(8,128)(2,1)S(1)} collective-permute-done((bf16[256,1024]{1,0:T(8,128)(2,1)}, bf16[256,1024]{1,0:T(8,128)(2,1)S(1)}, u32[]{:S(2)}, u32[]{:S(2)}) %collective-permute-start.13) | collective-permute-done | bytes 524320 | tf_op jit(solution)/shard_map/ppermute | solution.py:284
  75.3 13.2 %collective-permute-done.14.refs_3_ = bf16[256,1024]{1,0:T(8,128)(2,1)} collective-permute-done((bf16[256,1024]{1,0:T(8,128)(2,1)S(1)}, bf16[256,1024]{1,0:T(8,128)(2,1)}, u32[]{:S(2)}, u32[]{:S(2)}) %collective-permute-start.14) | collective-permute-done | bytes 524320 | tf_op jit(solution)/shard_map/ppermute | solution.py:288
  88.5 0.0 collective-permute-done.12.refs_0_
  88.5 3.1 %shard_map.66 = bf16[1024,256]{1,0:T(8,128)(2,1)} custom-call(s32[1]{0:T(128)} %bitcast.aux_ref, f32[256,1024]{1,0:T(8,128)S(1)} %get-tuple-element.42.total_ref, bf16[256,1024]{1,0:T(8,128)(2,1)} %collective-permute-done.12.refs_0_, bf16[256,1024]{1,0:T(8,128)(2,1)S(1)} %collective-permute-done.11.refs_5_.refs_1_, ...), custom_call_target="tpu_custom_call" | custom-call | tf_op jit(solution)/shard_map/pallas_call | solution.py:213
Async XLA Ops:
  0.7 8.8 %collective-permute-start = (bf16[8,1024]{1,0:T(8,128)(2,1)S(1)}, bf16[8,1024]{1,0:T(8,128)(2,1)S(1)}, u32[]{:S(2)}, u32[]{:S(2)}) collective-permute-start(bf16[8,1024]{1,0:T(8,128)(2,1)S(1)} %get-tuple-element.52), channel_id=1, source_target_pairs={{0,1},{1,0},{2,3},{3,2},{4,5},{5,4},{6,7},{7,6},{8,9},{9,8},{10,11... | collective-permute-start | bytes 49160 | tf_op jit(solution)/shard_map/ppermute | solution.py:23
  3.7 6.4 %collective-permute-start.1 = (bf16[8,1024]{1,0:T(8,128)(2,1)S(1)}, bf16[8,1024]{1,0:T(8,128)(2,1)S(1)}, u32[]{:S(2)}, u32[]{:S(2)}) collective-permute-start(bf16[8,1024]{1,0:T(8,128)(2,1)S(1)} %get-tuple-element.51), channel_id=1, source_target_pairs={{0,7},{1,2},{2,1},{3,4},{4,3},{5,6},{6,5},{7,0},{8,15},{9,10},{10,... | collective-permute-start | bytes 49160 | tf_op jit(solution)/shard_map/ppermute | solution.py:235
  17.2 1.9 %collective-permute-start.2 = (bf16[64,3840]{1,0:T(8,128)(2,1)S(1)}, bf16[64,3840]{1,0:T(8,128)(2,1)S(1)}, u32[]{:S(2)}, u32[]{:S(2)}) collective-permute-start(bf16[64,3840]{1,0:T(8,128)(2,1)S(1)} %get-tuple-element.29.refs_0_), channel_id=1, source_target_pairs={{0,8},{8,0},{16,24},{24,16},{1,9},{9,1},{17,25},{25,17},{2,10},{10... | collective-permute-start | bytes 1474568 | tf_op jit(solution)/shard_map/ppermute | solution.py:23
  17.3 13.6 %collective-permute-start.3 = (bf16[64,3840]{1,0:T(8,128)(2,1)S(1)}, bf16[64,3840]{1,0:T(8,128)(2,1)S(1)}, u32[]{:S(2)}, u32[]{:S(2)}) collective-permute-start(bf16[64,3840]{1,0:T(8,128)(2,1)S(1)} %get-tuple-element.29.refs_0_), channel_id=1, source_target_pairs={{0,16},{8,24},{16,0},{24,8},{1,17},{9,25},{17,1},{25,9},{2,18},{10... | collective-permute-start | bytes 1474568 | tf_op jit(solution)/shard_map/ppermute | solution.py:23
  22.5 8.4 %collective-permute-start.4 = (bf16[128,1024]{1,0:T(8,128)(2,1)S(1)}, bf16[128,1024]{1,0:T(8,128)(2,1)S(1)}, u32[]{:S(2)}, u32[]{:S(2)}) collective-permute-start(bf16[128,1024]{1,0:T(8,128)(2,1)S(1)} %get-tuple-element.32), channel_id=1, source_target_pairs={{0,1},{1,0},{2,3},{3,2},{4,5},{5,4},{6,7},{7,6},{8,9},{9,8},{10,11... | collective-permute-start | bytes 786440 | tf_op jit(solution)/shard_map/ppermute | solution.py:23
  30.9 1.9 %collective-permute-start.5 = (bf16[64,3840]{1,0:T(8,128)(2,1)S(1)}, bf16[64,3840]{1,0:T(8,128)(2,1)S(1)}, u32[]{:S(2)}, u32[]{:S(2)}) collective-permute-start(bf16[64,3840]{1,0:T(8,128)(2,1)S(1)} %collective-permute-done.3.refs_0_.refs_2_), channel_id=1, source_target_pairs={{0,8},{8,0},{16,24},{24,16},{1,9},{9,1},{17,25},{25,17},{2,10},{10... | collective-permute-start | bytes 1474568 | tf_op jit(solution)/shard_map/ppermute | solution.py:23
  30.9 10.8 %collective-permute-start.6 = (bf16[128,1024]{1,0:T(8,128)(2,1)S(1)}, bf16[128,1024]{1,0:T(8,128)(2,1)S(1)}, u32[]{:S(2)}, u32[]{:S(2)}) collective-permute-start(bf16[128,1024]{1,0:T(8,128)(2,1)S(1)} %get-tuple-element.36), channel_id=1, source_target_pairs={{0,1},{1,0},{2,3},{3,2},{4,5},{5,4},{6,7},{7,6},{8,9},{9,8},{10,11... | collective-permute-start | bytes 786440 | tf_op jit(solution)/shard_map/ppermute | solution.py:23
  36.2 9.7 %collective-permute-start.7 = (bf16[128,1024]{1,0:T(8,128)(2,1)S(1)}, bf16[128,1024]{1,0:T(8,128)(2,1)S(1)}, u32[]{:S(2)}, u32[]{:S(2)}) collective-permute-start(bf16[128,1024]{1,0:T(8,128)(2,1)S(1)} %get-tuple-element.38), channel_id=1, source_target_pairs={{0,1},{1,0},{2,3},{3,2},{4,5},{5,4},{6,7},{7,6},{8,9},{9,8},{10,11... | collective-permute-start | bytes 786440 | tf_op jit(solution)/shard_map/ppermute | solution.py:23
  40.0 12.5 %collective-permute-start.8 = (bf16[128,1024]{1,0:T(8,128)(2,1)S(1)}, bf16[128,1024]{1,0:T(8,128)(2,1)S(1)}, u32[]{:S(2)}, u32[]{:S(2)}) collective-permute-start(bf16[128,1024]{1,0:T(8,128)(2,1)S(1)} %get-tuple-element.40), channel_id=1, source_target_pairs={{0,1},{1,0},{2,3},{3,2},{4,5},{5,4},{6,7},{7,6},{8,9},{9,8},{10,11... | collective-permute-start | bytes 786440 | tf_op jit(solution)/shard_map/ppermute | solution.py:23
  45.6 17.2 %collective-permute-start.9 = (bf16[256,1024]{1,0:T(8,128)(2,1)S(1)}, bf16[256,1024]{1,0:T(8,128)(2,1)S(1)}, u32[]{:S(2)}, u32[]{:S(2)}) collective-permute-start(bf16[256,1024]{1,0:T(8,128)(2,1)S(1)} %get-tuple-element.44), channel_id=1, source_target_pairs={{0,1},{1,0},{2,3},{3,2},{4,5},{5,4},{6,7},{7,6},{8,9},{9,8},{10,11... | collective-permute-start | bytes 1572872 | tf_op jit(solution)/shard_map/ppermute | solution.py:23
  49.5 17.2 %collective-permute-start.10 = (bf16[256,1024]{1,0:T(8,128)(2,1)S(1)}, bf16[256,1024]{1,0:T(8,128)(2,1)S(1)}, u32[]{:S(2)}, u32[]{:S(2)}) collective-permute-start(bf16[256,1024]{1,0:T(8,128)(2,1)S(1)} %get-tuple-element.47), channel_id=1, source_target_pairs={{0,2},{1,3},{6,4},{7,5},{8,10},{9,11},{14,12},{15,13},{16,18},{17,... | collective-permute-start | bytes 1572872 | tf_op jit(solution)/shard_map/ppermute | solution.py:281
  51.6 15.4 %collective-permute-start.11 = (bf16[256,1024]{1,0:T(8,128)(2,1)S(1)}, bf16[256,1024]{1,0:T(8,128)(2,1)S(1)}, u32[]{:S(2)}, u32[]{:S(2)}) collective-permute-start(bf16[256,1024]{1,0:T(8,128)(2,1)S(1)} %get-tuple-element.47), channel_id=1, source_target_pairs={{2,4},{3,5},{4,2},{5,3},{10,12},{11,13},{12,10},{13,11},{18,20},{1... | collective-permute-start | bytes 1572872 | tf_op jit(solution)/shard_map/ppermute | solution.py:282
  56.9 18.4 %collective-permute-start.13 = (bf16[256,1024]{1,0:T(8,128)(2,1)}, bf16[256,1024]{1,0:T(8,128)(2,1)S(1)}, u32[]{:S(2)}, u32[]{:S(2)}) collective-permute-start(bf16[256,1024]{1,0:T(8,128)(2,1)} %get-tuple-element.48), channel_id=1, source_target_pairs={{0,4},{1,5},{6,2},{7,3},{2,0},{3,1},{4,6},{5,7},{8,12},{9,13},{14,... | collective-permute-start | bytes 1572872 | tf_op jit(solution)/shard_map/ppermute | solution.py:284
  66.8 21.7 %collective-permute-start.14 = (bf16[256,1024]{1,0:T(8,128)(2,1)S(1)}, bf16[256,1024]{1,0:T(8,128)(2,1)}, u32[]{:S(2)}, u32[]{:S(2)}) collective-permute-start(bf16[256,1024]{1,0:T(8,128)(2,1)S(1)} %add_convert_fusion.refs_4_), channel_id=1, source_target_pairs={{2,6},{3,7},{4,0},{5,1},{0,2},{1,3},{6,4},{7,5},{10,14},{11,15},{1... | collective-permute-start | bytes 1572872 | tf_op jit(solution)/shard_map/ppermute | solution.py:288
  70.6 17.9 %collective-permute-start.12 = (bf16[256,1024]{1,0:T(8,128)(2,1)S(1)}, bf16[256,1024]{1,0:T(8,128)(2,1)}, u32[]{:S(2)}, u32[]{:S(2)}) collective-permute-start(bf16[256,1024]{1,0:T(8,128)(2,1)S(1)} %shard_map.65), channel_id=1, source_target_pairs={{0,1},{1,0},{2,3},{3,2},{4,5},{5,4},{6,7},{7,6},{8,9},{9,8},{10,11... | collective-permute-start | bytes 1572872 | tf_op jit(solution)/shard_map/ppermute | solution.py:23
where the time goes:
time: 92 us; the launch traced here: 91.6 us
  Pallas kernels  46.7 us (51%)
  waiting for transfers between devices  23.9 us (26%)
  starting transfers between devices  17.7 us (19%)
  local copies, waits for them, and re-layouts  1.6 us (2%)
    pallas_call x10, Pallas kernels, product(): pl.pallas_call(functools.partial(product_kernel, step, kept, following, l...  36.6 us
    ppermute x1, waiting for transfers between devices, local(): lax.ppermute(sent, 'basis', along([(1, 3), (2, 0), (0, 1), (3, 2)]))  13.2 us
    ppermute x10, starting transfers between devices, exchange(): return lax.ppermute(array, axis, [(i, i ^ bit) for i in range(peers)])  8.88 us
    pallas_call x1, Pallas kernels, half_rows(): pl.pallas_call(functools.partial(half_kernel, groups, blocks, following),...  7.05 us
    ppermute x10, waiting for transfers between devices, exchange(): return lax.ppermute(array, axis, [(i, i ^ bit) for i in range(peers)])  6.81 us
    ppermute x1, starting transfers between devices, local(): after = lax.ppermute(jnp.where(even, first, last), 'basis', ring)  3.54 us
    ppermute x1, waiting for transfers between devices, local(): third = lax.ppermute(sent, 'basis', along([(0, 2), (3, 1), (1, 0), (2, 3)]))  3.25 us
    pallas_call x1, Pallas kernels, finish(): pl.pallas_call(functools.partial(finish_kernel, slab, tuple((len(add) for...  3.09 us
  transfers between devices with their start and end apart: 15, of which 6 were waited for; matrix products, arithmetic and copies ran while one was open for 2% of the time, Pallas kernels for 40%

commit v1 on v0

--- a/solution.py
+++ b/solution.py
@@ -203,9 +203,11 @@
         total += joined(add_refs[at : at + count])
         at += count
     acc_ref[...] = total
-    for s in range(acc_ref.shape[0] // slab):
-        rows = acc_ref[pl.ds(pl.multiple_of((aux_ref[0] ^ s) * slab, slab), slab), :]
-        out_ref[:, s * slab : (s + 1) * slab] = rows.T.astype(BF16)
+    ordered = [
+        acc_ref[pl.ds(pl.multiple_of((aux_ref[0] ^ s) * slab, slab), slab), :]
+        for s in range(acc_ref.shape[0] // slab)
+    ]
+    out_ref[...] = jnp.concatenate(ordered, axis=0).T.astype(BF16)
 
 
 def finish(aux, total, adds, slab):
@@ -242,9 +244,9 @@
     sends = [(m, False) for m in (top, second)]
     keeps = [(m, True) for m in (top, second, *others)]
     if groups == 4:
-        order = [*sends, *sends, (THIRD, False), *keeps[:2], keeps[3], keeps[2], (0, False)]
+        order = [sends[0], (THIRD, False), *sends, keeps[0], (THIRD, False), keeps[1], keeps[3], keeps[2], (0, False)]
     else:
-        order = [*sends, *sends, *((m, False) for m in others), *keeps]
+        order = [sends[0], *sends, *((m, False) for m in others), *keeps]
     number = basis.reshape(1)
     own, first = half_rows(
         number, pair_map, pair_count, table, pair, after, v_blocks, virt_coef, blocks, width, order[0]
@@ -268,18 +270,19 @@
         bit //= 2
     far = far[1:]
     received = {top: (send(top, early),)}
-    received[second] = (send(second, early),)
+    if groups == 4:
+        received[THIRD] = (send(THIRD, early),)
     *far, _, _ = lax.optimization_barrier((*far, carry[0], received[top][0]))
     late = [block for rows in far for block in (rows, exchange(rows, "aux", 1))]
     every = early + late
     received[top] += (send(top, late),)
-    received[second] += (send(second, late),)
+    received[second] = (send(second, every, after=received.get(THIRD, ())),)
     if groups == 4:
-        received[THIRD] = (send(THIRD, every, received[SECOND][:1]),)
         sent = mult(3, True, every, (received[3],))
         along = lambda pairs: [(2 * a + s, 2 * b + s) for a, b in pairs for s in (0, 1)]
         relayed = lax.ppermute(sent, "basis", along([(0, 1), (3, 2)]))
         inner = lax.ppermute(sent, "basis", along([(1, 2), (2, 1)]))
+        received[THIRD] += (send(THIRD, late),)
         sent = mult(SECOND, True, every, (received[SECOND],))
         third = lax.ppermute(sent, "basis", along([(0, 2), (3, 1), (1, 0), (2, 3)]))
         total = mult(0, True, every, dtype=F32)
@@ -287,8 +290,9 @@
         sent = (part + relayed.astype(F32)).astype(BF16)
         fourth = lax.ppermute(sent, "basis", along([(1, 3), (2, 0), (0, 1), (3, 2)]))
         received[0] = (send(0, every, after=(sent, inner)),)
-        third, fourth = lax.optimization_barrier((third, fourth))
-        adds = (received[0], (inner,), (third,), (fourth,))
+        total = total + inner.astype(F32) + third.astype(F32)
+        total, fourth = lax.optimization_barrier((total, fourth))
+        adds = (received[0], (fourth,))
     else:
         for m in others:
             received[m] = (send(m, every),)

time: 92 us -> 89.9 us (0.977)
  starting transfers between devices: 17.7 us -> 15.8 us
  other arithmetic: 0.89 us -> 2.16 us
    ppermute x10, waiting for transfers between devices: 6.81 us -> 13.8 us  [exchange(): return lax.ppermute(array, axis, [(i, i ^ bit) for i in range(peers)])]
    ppermute x1, waiting for transfers between devices: 13.2 us -> 9.46 us  [local(): lax.ppermute(sent, 'basis', along([(1, 3), (2, 0), (0, 1), (3, 2)]))]
    ppermute x10, starting transfers between devices: 8.88 us -> 5.43 us  [exchange(): return lax.ppermute(array, axis, [(i, i ^ bit) for i in range(peers)])]
    ppermute x1, waiting for transfers between devices: 3.25 us -> 0.01 us  [local(): third = lax.ppermute(sent, 'basis', along([(0, 2), (3, 1), (1, 0), (2, 3)]))]
    ppermute x1, starting transfers between devices: 3.54 us -> 6 us  [local(): after = lax.ppermute(jnp.where(even, first, last), 'basis', ring)]
    ppermute x1, starting transfers between devices: 2.08 us -> 0.06 us  [local(): third = lax.ppermute(sent, 'basis', along([(0, 2), (3, 1), (1, 0), (2, 3)]))]
    ppermute x1, starting transfers between devices: 0.18 us -> 2.07 us  [local(): lax.ppermute(sent, 'basis', along([(1, 3), (2, 0), (0, 1), (3, 2)]))]
    add x0 -> x1, other arithmetic: none -> 1.25 us  [local(): total = total + inner.astype(F32) + third.astype(F32)]
  transfers between devices with their start and end apart: 15 -> 15, of which waited for: 6 -> 9; matrix products, arithmetic and copies ran while one was open for 2% -> 3% of each run, Pallas kernels for 40% -> 41%
where the time goes in v1:
time: 89.9 us; the launch traced here: 89.6 us
  Pallas kernels  45.9 us (51%)
  waiting for transfers between devices  23.3 us (26%)
  starting transfers between devices  15.8 us (18%)
  other arithmetic  2.16 us (2%)
  local copies, waits for them, and re-layouts  1.6 us (2%)
    pallas_call x10, Pallas kernels, product(): pl.pallas_call(functools.partial(product_kernel, step, kept, following, l...  36.6 us
    ppermute x10, waiting for transfers between devices, exchange(): return lax.ppermute(array, axis, [(i, i ^ bit) for i in range(peers)])  13.8 us
    ppermute x1, waiting for transfers between devices, local(): lax.ppermute(sent, 'basis', along([(1, 3), (2, 0), (0, 1), (3, 2)]))  9.46 us
    pallas_call x1, Pallas kernels, half_rows(): pl.pallas_call(functools.partial(half_kernel, groups, blocks, following),...  7.05 us
    ppermute x1, starting transfers between devices, local(): after = lax.ppermute(jnp.where(even, first, last), 'basis', ring)  6 us
    ppermute x10, starting transfers between devices, exchange(): return lax.ppermute(array, axis, [(i, i ^ bit) for i in range(peers)])  5.43 us
    pallas_call x1, Pallas kernels, finish(): pl.pallas_call(functools.partial(finish_kernel, slab, tuple((len(add) for...  2.27 us
    ppermute x1, starting transfers between devices, local(): lax.ppermute(sent, 'basis', along([(1, 3), (2, 0), (0, 1), (3, 2)]))  2.07 us
  transfers between devices with their start and end apart: 15, of which 9 were waited for; matrix products, arithmetic and copies ran while one was open for 3% of the time, Pallas kernels for 41%

profile of v1, /device:TPU:0, one launch (start us, length us, event | category | flops | bytes accessed | tf_op | source)
XLA Modules:
  0.0 89.6 jit_solution(10221494830580112096)
XLA Ops:
  0.0 0.7 broadcast_select_fusion
  0.7 6.0 %collective-permute-start.1 = (bf16[8,1024]{1,0:T(8,128)(2,1)S(1)}, bf16[8,1024]{1,0:T(8,128)(2,1)S(1)}, u32[]{:S(2)}, u32[]{:S(2)}) collective-permute-start(bf16[8,1024]{1,0:T(8,128)(2,1)S(1)} %get-tuple-element.51), channel_id=1, source_target_pairs={{0,7},{1,2},{2,1},{3,4},{4,3},{5,6},{6,5},{7,0},{8,15},{9,10},{10,... | collective-permute-start | bytes 49160 | tf_op jit(solution)/shard_map/ppermute | solution.py:237
  6.7 0.0 collective-permute-start
  7.4 0.8 copy.6.map_ref
  8.2 0.8 pad.4.table_ref
  9.0 0.0 collective-permute-done.1.next_ref
  9.0 1.5 %collective-permute-done.pair_ref = bf16[8,1024]{1,0:T(8,128)(2,1)S(1)} collective-permute-done((bf16[8,1024]{1,0:T(8,128)(2,1)S(1)}, bf16[8,1024]{1,0:T(8,128)(2,1)S(1)}, u32[]{:S(2)}, u32[]{:S(2)}) %collective-permute-start) | collective-permute-done | bytes 16416 | tf_op jit(solution)/shard_map/ppermute | solution.py:23
  10.5 7.0 %shard_map.55 = (bf16[64,3840]{1,0:T(8,128)(2,1)S(1)}, bf16[768,1024]{1,0:T(8,128)(2,1)S(1)}) custom-call(s32[1]{0:T(128)} %bitcast.1.basis_ref, s32[1,48,2]{2,1,0:T(8,128)S(1)} %copy.6.map_ref, s32[1,1]{1,0:T(1,128)S(6)} %copy.7.count_ref, bf16[8,5888]{1,0:T(8,128)(2,1)S(1)} %pad.4.table_ref, bf16[8,1024]{1,0:T(8,128)(2,1)S(1)} %collective-permute-done.pair_ref, ...), custom_call_target="tpu_custom_call" | custom-call | flops 100663296 | bytes 12582912 | tf_op jit(solution)/shard_map/pallas_call | solution.py:96
  17.5 0.1 collective-permute-start.2
  17.6 1.6 %collective-permute-start.3 = (bf16[64,3840]{1,0:T(8,128)(2,1)S(1)}, bf16[64,3840]{1,0:T(8,128)(2,1)S(1)}, u32[]{:S(2)}, u32[]{:S(2)}) collective-permute-start(bf16[64,3840]{1,0:T(8,128)(2,1)S(1)} %get-tuple-element.29.refs_0_), channel_id=1, source_target_pairs={{0,16},{8,24},{16,0},{24,8},{1,17},{9,25},{17,1},{25,9},{2,18},{10... | collective-permute-start | bytes 1474568 | tf_op jit(solution)/shard_map/ppermute | solution.py:23
  19.2 0.3 collective-permute-done.2.refs_1_
  19.5 3.4 %shard_map.56 = (bf16[128,1024]{1,0:T(8,128)(2,1)S(1)}, bf16[768,1024]{1,0:T(8,128)(2,1)S(1)}) custom-call(s32[1]{0:T(128)} %bitcast.1.basis_ref, bf16[3840,8192]{1,0:T(8,128)(2,1)} %virt_ref.21, bf16[768,1024]{1,0:T(8,128)(2,1)S(1)} %get-tuple-element.28.first_ref, bf16[64,3840]{1,0:T(8,128)(2,1)S(1)} %get-tuple-element.29.refs_0_, ...), custom_call_target="tpu_custom_call" | custom-call | flops 1006632960 | bytes 7864320 | tf_op jit(solution)/shard_map/pallas_call | solution.py:181
  22.9 0.6 collective-permute-start.4
  23.5 3.4 %shard_map.57 = (bf16[128,1024]{1,0:T(8,128)(2,1)S(1)}, bf16[768,1024]{1,0:T(8,128)(2,1)S(1)}) custom-call(s32[1]{0:T(128)} %bitcast.1.basis_ref, bf16[3840,8192]{1,0:T(8,128)(2,1)} %virt_ref.21, bf16[768,1024]{1,0:T(8,128)(2,1)S(1)} %get-tuple-element.30.first_ref, bf16[64,3840]{1,0:T(8,128)(2,1)S(1)} %get-tuple-element.29.refs_0_, ...), custom_call_target="tpu_custom_call" | custom-call | flops 1006632960 | bytes 7864320 | tf_op jit(solution)/shard_map/pallas_call | solution.py:181
  26.9 4.4 %collective-permute-done.3.refs_0_.refs_2_ = bf16[64,3840]{1,0:T(8,128)(2,1)S(1)} collective-permute-done((bf16[64,3840]{1,0:T(8,128)(2,1)S(1)}, bf16[64,3840]{1,0:T(8,128)(2,1)S(1)}, u32[]{:S(2)}, u32[]{:S(2)}) %collective-permute-start.3) | collective-permute-done | bytes 491552 | tf_op jit(solution)/shard_map/ppermute | solution.py:23
  31.3 0.0 collective-permute-done.4.refs_4_
  31.3 0.0 collective-permute-start.5
  31.3 0.6 collective-permute-start.6
  31.9 1.3 %collective-permute-done.5.refs_1_.refs_3_ = bf16[64,3840]{1,0:T(8,128)(2,1)S(1)} collective-permute-done((bf16[64,3840]{1,0:T(8,128)(2,1)S(1)}, bf16[64,3840]{1,0:T(8,128)(2,1)S(1)}, u32[]{:S(2)}, u32[]{:S(2)}) %collective-permute-start.5) | collective-permute-done | bytes 491552 | tf_op jit(solution)/shard_map/ppermute | solution.py:23
  33.1 3.4 %shard_map.58 = (bf16[128,1024]{1,0:T(8,128)(2,1)S(1)}, bf16[768,1024]{1,0:T(8,128)(2,1)S(1)}) custom-call(s32[1]{0:T(128)} %bitcast.1.basis_ref, bf16[3840,8192]{1,0:T(8,128)(2,1)} %virt_ref.21, bf16[768,1024]{1,0:T(8,128)(2,1)S(1)} %get-tuple-element.31.first_ref, bf16[64,3840]{1,0:T(8,128)(2,1)S(1)} %collective-permute-done.3.refs_0_.refs_2_, ...), custom_call_target="tpu_custom_call" | custom-call | flops 1006632960 | bytes 7864320 | tf_op jit(solution)/shard_map/pallas_call | solution.py:181
  36.5 0.6 collective-permute-start.7
  37.2 3.2 %collective-permute-done.6.refs_4_ = bf16[128,1024]{1,0:T(8,128)(2,1)S(1)} collective-permute-done((bf16[128,1024]{1,0:T(8,128)(2,1)S(1)}, bf16[128,1024]{1,0:T(8,128)(2,1)S(1)}, u32[]{:S(2)}, u32[]{:S(2)}) %collective-permute-start.6) | collective-permute-done | bytes 262176 | tf_op jit(solution)/shard_map/ppermute | solution.py:23
  40.4 3.8 %shard_map.59 = (bf16[256,1024]{1,0:T(8,128)(2,1)S(1)}, bf16[768,1024]{1,0:T(8,128)(2,1)S(1)}) custom-call(s32[1]{0:T(128)} %bitcast.1.basis_ref, bf16[3840,8192]{1,0:T(8,128)(2,1)} %virt_ref.21, bf16[768,1024]{1,0:T(8,128)(2,1)S(1)} %get-tuple-element.34.first_ref, bf16[64,3840]{1,0:T(8,128)(2,1)S(1)} %get-tuple-element.29.refs_0_, ...), custom_call_target="tpu_custom_call" | custom-call | flops 2013265920 | bytes 7864320 | tf_op jit(solution)/shard_map/pallas_call | solution.py:181
  44.2 0.6 collective-permute-start.8
  44.8 0.8 collective-permute-done.7.refs_5_
  45.6 3.6 %shard_map.60 = (bf16[256,1024]{1,0:T(8,128)(2,1)S(1)}, bf16[768,1024]{1,0:T(8,128)(2,1)S(1)}) custom-call(s32[1]{0:T(128)} %bitcast.1.basis_ref, bf16[3840,8192]{1,0:T(8,128)(2,1)} %virt_ref.21, bf16[768,1024]{1,0:T(8,128)(2,1)S(1)} %get-tuple-element.36.first_ref, bf16[64,3840]{1,0:T(8,128)(2,1)S(1)} %get-tuple-element.29.refs_0_, ...), custom_call_target="tpu_custom_call" | custom-call | flops 2013265920 | bytes 7864320 | tf_op jit(solution)/shard_map/pallas_call | solution.py:181
  49.2 1.3 %collective-permute-start.12 = (bf16[256,1024]{1,0:T(8,128)(2,1)S(1)}, bf16[256,1024]{1,0:T(8,128)(2,1)S(1)}, u32[]{:S(2)}, u32[]{:S(2)}) collective-permute-start(bf16[256,1024]{1,0:T(8,128)(2,1)S(1)} %get-tuple-element.43), channel_id=1, source_target_pairs={{0,2},{1,3},{6,4},{7,5},{8,10},{9,11},{14,12},{15,13},{16,18},{17,... | collective-permute-start | bytes 1572872 | tf_op jit(solution)/shard_map/ppermute | solution.py:283
  50.6 0.9 collective-permute-start.9
  51.5 3.4 %shard_map.61 = (bf16[128,1024]{1,0:T(8,128)(2,1)S(1)}, bf16[768,1024]{1,0:T(8,128)(2,1)S(1)}) custom-call(s32[1]{0:T(128)} %bitcast.1.basis_ref, bf16[3840,8192]{1,0:T(8,128)(2,1)} %virt_ref.21, bf16[768,1024]{1,0:T(8,128)(2,1)S(1)} %get-tuple-element.38.first_ref, bf16[64,3840]{1,0:T(8,128)(2,1)S(1)} %collective-permute-done.3.refs_0_.refs_2_, ...), custom_call_target="tpu_custom_call" | custom-call | flops 1006632960 | bytes 7864320 | tf_op jit(solution)/shard_map/pallas_call | solution.py:181
  54.9 0.8 collective-permute-start.11
  55.6 2.0 %collective-permute-done.8.refs_4_ = bf16[256,1024]{1,0:T(8,128)(2,1)S(1)} collective-permute-done((bf16[256,1024]{1,0:T(8,128)(2,1)S(1)}, bf16[256,1024]{1,0:T(8,128)(2,1)S(1)}, u32[]{:S(2)}, u32[]{:S(2)}) %collective-permute-start.8) | collective-permute-done | bytes 524320 | tf_op jit(solution)/shard_map/ppermute | solution.py:23
  57.6 4.4 %shard_map.62 = (bf16[256,1024]{1,0:T(8,128)(2,1)}, bf16[768,1024]{1,0:T(8,128)(2,1)S(1)}) custom-call(s32[1]{0:T(128)} %bitcast.1.basis_ref, bf16[3840,8192]{1,0:T(8,128)(2,1)} %virt_ref.21, bf16[768,1024]{1,0:T(8,128)(2,1)S(1)} %get-tuple-element.39.first_ref, bf16[64,3840]{1,0:T(8,128)(2,1)S(1)} %get-tuple-element.29.refs_0_, ...), custom_call_target="tpu_custom_call" | custom-call | flops 2013265920 | bytes 7864320 | tf_op jit(solution)/shard_map/pallas_call | solution.py:181
  62.0 0.1 collective-permute-start.10
  62.0 3.8 %shard_map.63 = (f32[256,1024]{1,0:T(8,128)S(1)}, bf16[768,1024]{1,0:T(8,128)(2,1)S(1)}) custom-call(s32[1]{0:T(128)} %bitcast.1.basis_ref, bf16[3840,8192]{1,0:T(8,128)(2,1)} %virt_ref.21, bf16[768,1024]{1,0:T(8,128)(2,1)S(1)} %get-tuple-element.41.first_ref, bf16[64,3840]{1,0:T(8,128)(2,1)S(1)} %get-tuple-element.29.refs_0_, ...), custom_call_target="tpu_custom_call" | custom-call | flops 2013265920 | bytes 7864320 | tf_op jit(solution)/shard_map/pallas_call | solution.py:181
  65.9 0.0 collective-permute-done.11.refs_5_
  65.9 3.8 %shard_map.64 = (f32[256,1024]{1,0:T(8,128)S(1)}, bf16[768,1024]{1,0:T(8,128)(2,1)S(1)}) custom-call(s32[1]{0:T(128)} %bitcast.1.basis_ref, bf16[3840,8192]{1,0:T(8,128)(2,1)} %virt_ref.21, bf16[768,1024]{1,0:T(8,128)(2,1)S(1)} %get-tuple-element.45.first_ref, bf16[64,3840]{1,0:T(8,128)(2,1)S(1)} %get-tuple-element.29.refs_0_, ...), custom_call_target="tpu_custom_call" | custom-call | flops 2013265920 | bytes 7864320 | tf_op jit(solution)/shard_map/pallas_call | solution.py:181
  69.7 0.0 collective-permute-done.12
  69.7 0.2 add_convert_fusion.refs_4_
  69.9 2.1 %collective-permute-start.13 = (bf16[256,1024]{1,0:T(8,128)(2,1)S(1)}, bf16[256,1024]{1,0:T(8,128)(2,1)S(1)}, u32[]{:S(2)}, u32[]{:S(2)}) collective-permute-start(bf16[256,1024]{1,0:T(8,128)(2,1)S(1)} %add_convert_fusion.refs_4_), channel_id=1, source_target_pairs={{2,6},{3,7},{4,0},{5,1},{0,2},{1,3},{6,4},{7,5},{10,14},{11,15},{1... | collective-permute-start | bytes 1572872 | tf_op jit(solution)/shard_map/ppermute | solution.py:291
  72.0 0.0 collective-permute-done.9.refs_5_
  72.0 3.6 %shard_map.65 = bf16[256,1024]{1,0:T(8,128)(2,1)S(1)} custom-call(s32[1]{0:T(128)} %bitcast.1.basis_ref, bf16[3840,8192]{1,0:T(8,128)(2,1)} %virt_ref.21, bf16[768,1024]{1,0:T(8,128)(2,1)S(1)} %get-tuple-element.49.first_ref, bf16[64,3840]{1,0:T(8,128)(2,1)S(1)} %get-tuple-element.29.refs_0_, bf16[64,3840]{1,0:T(8,128)(2,1)S(1)} %collective-permute-done.2.refs_1_, ...), custom_call_target="tpu_custom_call" | custom-call | flops 2013265920 | bytes 7864320 | tf_op jit(solution)/shard_map/pallas_call | solution.py:181
  75.6 0.6 collective-permute-start.14
  76.2 0.0 collective-permute-done.10
  76.2 1.3 %convert_add_fusion.total_ref = f32[256,1024]{1,0:T(8,128)S(1)} fusion(bf16[256,1024]{1,0:T(8,128)(2,1)} %collective-permute-done.10, f32[256,1024]{1,0:T(8,128)S(1)} %get-tuple-element.42, bf16[256,1024]{1,0:T(8,128)(2,1)S(1)} %collective-permute-done.9.refs_5_), kind=kLoop, calls=%fused_computation.1 | loop fusion | flops 1048576 | bytes 3145728 | tf_op jit(solution)/shard_map/add | solution.py:293
  77.5 9.5 %collective-permute-done.13.refs_1_ = bf16[256,1024]{1,0:T(8,128)(2,1)S(1)} collective-permute-done((bf16[256,1024]{1,0:T(8,128)(2,1)S(1)}, bf16[256,1024]{1,0:T(8,128)(2,1)S(1)}, u32[]{:S(2)}, u32[]{:S(2)}) %collective-permute-start.13) | collective-permute-done | bytes 524320 | tf_op jit(solution)/shard_map/ppermute | solution.py:291
  86.9 0.4 collective-permute-done.14.refs_0_
  87.3 2.3 %shard_map.66 = bf16[1024,256]{1,0:T(8,128)(2,1)} custom-call(s32[1]{0:T(128)} %bitcast.aux_ref, f32[256,1024]{1,0:T(8,128)S(1)} %convert_add_fusion.total_ref, bf16[256,1024]{1,0:T(8,128)(2,1)} %collective-permute-done.14.refs_0_, bf16[256,1024]{1,0:T(8,128)(2,1)S(1)} %collective-permute-done.13.refs_1_), custom_call_target="tpu_custom_call" | custom-call | tf_op jit(solution)/shard_map/pallas_call | solution.py:215
Async XLA Ops:
  0.7 8.3 %collective-permute-start.1 = (bf16[8,1024]{1,0:T(8,128)(2,1)S(1)}, bf16[8,1024]{1,0:T(8,128)(2,1)S(1)}, u32[]{:S(2)}, u32[]{:S(2)}) collective-permute-start(bf16[8,1024]{1,0:T(8,128)(2,1)S(1)} %get-tuple-element.51), channel_id=1, source_target_pairs={{0,7},{1,2},{2,1},{3,4},{4,3},{5,6},{6,5},{7,0},{8,15},{9,10},{10,... | collective-permute-start | bytes 49160 | tf_op jit(solution)/shard_map/ppermute | solution.py:237
  6.7 3.7 %collective-permute-start = (bf16[8,1024]{1,0:T(8,128)(2,1)S(1)}, bf16[8,1024]{1,0:T(8,128)(2,1)S(1)}, u32[]{:S(2)}, u32[]{:S(2)}) collective-permute-start(bf16[8,1024]{1,0:T(8,128)(2,1)S(1)} %get-tuple-element.52), channel_id=1, source_target_pairs={{0,1},{1,0},{2,3},{3,2},{4,5},{5,4},{6,7},{7,6},{8,9},{9,8},{10,11... | collective-permute-start | bytes 49160 | tf_op jit(solution)/shard_map/ppermute | solution.py:23
  17.5 1.9 %collective-permute-start.2 = (bf16[64,3840]{1,0:T(8,128)(2,1)S(1)}, bf16[64,3840]{1,0:T(8,128)(2,1)S(1)}, u32[]{:S(2)}, u32[]{:S(2)}) collective-permute-start(bf16[64,3840]{1,0:T(8,128)(2,1)S(1)} %get-tuple-element.29.refs_0_), channel_id=1, source_target_pairs={{0,8},{8,0},{16,24},{24,16},{1,9},{9,1},{17,25},{25,17},{2,10},{10... | collective-permute-start | bytes 1474568 | tf_op jit(solution)/shard_map/ppermute | solution.py:23
  17.6 13.6 %collective-permute-start.3 = (bf16[64,3840]{1,0:T(8,128)(2,1)S(1)}, bf16[64,3840]{1,0:T(8,128)(2,1)S(1)}, u32[]{:S(2)}, u32[]{:S(2)}) collective-permute-start(bf16[64,3840]{1,0:T(8,128)(2,1)S(1)} %get-tuple-element.29.refs_0_), channel_id=1, source_target_pairs={{0,16},{8,24},{16,0},{24,8},{1,17},{9,25},{17,1},{25,9},{2,18},{10... | collective-permute-start | bytes 1474568 | tf_op jit(solution)/shard_map/ppermute | solution.py:23
  22.9 8.4 %collective-permute-start.4 = (bf16[128,1024]{1,0:T(8,128)(2,1)S(1)}, bf16[128,1024]{1,0:T(8,128)(2,1)S(1)}, u32[]{:S(2)}, u32[]{:S(2)}) collective-permute-start(bf16[128,1024]{1,0:T(8,128)(2,1)S(1)} %get-tuple-element.32), channel_id=1, source_target_pairs={{0,1},{1,0},{2,3},{3,2},{4,5},{5,4},{6,7},{7,6},{8,9},{9,8},{10,11... | collective-permute-start | bytes 786440 | tf_op jit(solution)/shard_map/ppermute | solution.py:23
  31.3 1.9 %collective-permute-start.5 = (bf16[64,3840]{1,0:T(8,128)(2,1)S(1)}, bf16[64,3840]{1,0:T(8,128)(2,1)S(1)}, u32[]{:S(2)}, u32[]{:S(2)}) collective-permute-start(bf16[64,3840]{1,0:T(8,128)(2,1)S(1)} %collective-permute-done.3.refs_0_.refs_2_), channel_id=1, source_target_pairs={{0,8},{8,0},{16,24},{24,16},{1,9},{9,1},{17,25},{25,17},{2,10},{10... | collective-permute-start | bytes 1474568 | tf_op jit(solution)/shard_map/ppermute | solution.py:23
  31.3 9.1 %collective-permute-start.6 = (bf16[128,1024]{1,0:T(8,128)(2,1)S(1)}, bf16[128,1024]{1,0:T(8,128)(2,1)S(1)}, u32[]{:S(2)}, u32[]{:S(2)}) collective-permute-start(bf16[128,1024]{1,0:T(8,128)(2,1)S(1)} %get-tuple-element.35), channel_id=1, source_target_pairs={{0,1},{1,0},{2,3},{3,2},{4,5},{5,4},{6,7},{7,6},{8,9},{9,8},{10,11... | collective-permute-start | bytes 786440 | tf_op jit(solution)/shard_map/ppermute | solution.py:23
  36.5 9.1 %collective-permute-start.7 = (bf16[128,1024]{1,0:T(8,128)(2,1)S(1)}, bf16[128,1024]{1,0:T(8,128)(2,1)S(1)}, u32[]{:S(2)}, u32[]{:S(2)}) collective-permute-start(bf16[128,1024]{1,0:T(8,128)(2,1)S(1)} %get-tuple-element.37), channel_id=1, source_target_pairs={{0,1},{1,0},{2,3},{3,2},{4,5},{5,4},{6,7},{7,6},{8,9},{9,8},{10,11... | collective-permute-start | bytes 786440 | tf_op jit(solution)/shard_map/ppermute | solution.py:23
  44.2 13.4 %collective-permute-start.8 = (bf16[256,1024]{1,0:T(8,128)(2,1)S(1)}, bf16[256,1024]{1,0:T(8,128)(2,1)S(1)}, u32[]{:S(2)}, u32[]{:S(2)}) collective-permute-start(bf16[256,1024]{1,0:T(8,128)(2,1)S(1)} %get-tuple-element.40), channel_id=1, source_target_pairs={{0,1},{1,0},{2,3},{3,2},{4,5},{5,4},{6,7},{7,6},{8,9},{9,8},{10,11... | collective-permute-start | bytes 1572872 | tf_op jit(solution)/shard_map/ppermute | solution.py:23
  49.2 20.5 %collective-permute-start.12 = (bf16[256,1024]{1,0:T(8,128)(2,1)S(1)}, bf16[256,1024]{1,0:T(8,128)(2,1)S(1)}, u32[]{:S(2)}, u32[]{:S(2)}) collective-permute-start(bf16[256,1024]{1,0:T(8,128)(2,1)S(1)} %get-tuple-element.43), channel_id=1, source_target_pairs={{0,2},{1,3},{6,4},{7,5},{8,10},{9,11},{14,12},{15,13},{16,18},{17,... | collective-permute-start | bytes 1572872 | tf_op jit(solution)/shard_map/ppermute | solution.py:283
  50.6 21.4 %collective-permute-start.9 = (bf16[256,1024]{1,0:T(8,128)(2,1)S(1)}, bf16[256,1024]{1,0:T(8,128)(2,1)S(1)}, u32[]{:S(2)}, u32[]{:S(2)}) collective-permute-start(bf16[256,1024]{1,0:T(8,128)(2,1)S(1)} %get-tuple-element.43), channel_id=1, source_target_pairs={{2,4},{3,5},{4,2},{5,3},{10,12},{11,13},{12,10},{13,11},{18,20},{1... | collective-permute-start | bytes 1572872 | tf_op jit(solution)/shard_map/ppermute | solution.py:284
  54.9 11.0 %collective-permute-start.11 = (bf16[128,1024]{1,0:T(8,128)(2,1)S(1)}, bf16[128,1024]{1,0:T(8,128)(2,1)S(1)}, u32[]{:S(2)}, u32[]{:S(2)}) collective-permute-start(bf16[128,1024]{1,0:T(8,128)(2,1)S(1)} %get-tuple-element.46), channel_id=1, source_target_pairs={{0,1},{1,0},{2,3},{3,2},{4,5},{5,4},{6,7},{7,6},{8,9},{9,8},{10,11... | collective-permute-start | bytes 786440 | tf_op jit(solution)/shard_map/ppermute | solution.py:23
  62.0 14.2 %collective-permute-start.10 = (bf16[256,1024]{1,0:T(8,128)(2,1)}, bf16[256,1024]{1,0:T(8,128)(2,1)}, u32[]{:S(2)}, u32[]{:S(2)}) collective-permute-start(bf16[256,1024]{1,0:T(8,128)(2,1)} %get-tuple-element.44), channel_id=1, source_target_pairs={{0,4},{1,5},{6,2},{7,3},{2,0},{3,1},{4,6},{5,7},{8,12},{9,13},{14,... | collective-permute-start | bytes 1572872 | tf_op jit(solution)/shard_map/ppermute | solution.py:287
  69.9 17.0 %collective-permute-start.13 = (bf16[256,1024]{1,0:T(8,128)(2,1)S(1)}, bf16[256,1024]{1,0:T(8,128)(2,1)S(1)}, u32[]{:S(2)}, u32[]{:S(2)}) collective-permute-start(bf16[256,1024]{1,0:T(8,128)(2,1)S(1)} %add_convert_fusion.refs_4_), channel_id=1, source_target_pairs={{2,6},{3,7},{4,0},{5,1},{0,2},{1,3},{6,4},{7,5},{10,14},{11,15},{1... | collective-permute-start | bytes 1572872 | tf_op jit(solution)/shard_map/ppermute | solution.py:291
  75.6 11.7 %collective-permute-start.14 = (bf16[256,1024]{1,0:T(8,128)(2,1)S(1)}, bf16[256,1024]{1,0:T(8,128)(2,1)}, u32[]{:S(2)}, u32[]{:S(2)}) collective-permute-start(bf16[256,1024]{1,0:T(8,128)(2,1)S(1)} %shard_map.65), channel_id=1, source_target_pairs={{0,1},{1,0},{2,3},{3,2},{4,5},{5,4},{6,7},{7,6},{8,9},{9,8},{10,11... | collective-permute-start | bytes 1572872 | tf_op jit(solution)/shard_map/ppermute | solution.py:23

commit v2 on v1

--- a/solution.py
+++ b/solution.py
@@ -244,7 +244,7 @@
     sends = [(m, False) for m in (top, second)]
     keeps = [(m, True) for m in (top, second, *others)]
     if groups == 4:
-        order = [sends[0], (THIRD, False), *sends, keeps[0], (THIRD, False), keeps[1], keeps[3], keeps[2], (0, False)]
+        order = [sends[0], (THIRD, False), *sends, keeps[0], (THIRD, False), *keeps[1:3], (0, False), keeps[3]]
     else:
         order = [sends[0], *sends, *((m, False) for m in others), *keeps]
     number = basis.reshape(1)
@@ -285,11 +285,11 @@
         received[THIRD] += (send(THIRD, late),)
         sent = mult(SECOND, True, every, (received[SECOND],))
         third = lax.ppermute(sent, "basis", along([(0, 2), (3, 1), (1, 0), (2, 3)]))
-        total = mult(0, True, every, dtype=F32)
-        part = mult(THIRD, True, every, (received[THIRD],), dtype=F32)
+        part = mult(THIRD, True, every, (received[THIRD],), after=(inner,), dtype=F32)
         sent = (part + relayed.astype(F32)).astype(BF16)
         fourth = lax.ppermute(sent, "basis", along([(1, 3), (2, 0), (0, 1), (3, 2)]))
-        received[0] = (send(0, every, after=(sent, inner)),)
+        received[0] = (send(0, every, after=(sent,)),)
+        total = mult(0, True, every, dtype=F32)
         total = total + inner.astype(F32) + third.astype(F32)
         total, fourth = lax.optimization_barrier((total, fourth))
         adds = (received[0], (fourth,))

time: 89.9 us -> 91 us (1.012)
  waiting for transfers between devices: 23.3 us -> 19.4 us
  local copies, waits for them, and re-layouts: 1.6 us -> 4.18 us
  starting transfers between devices: 15.8 us -> 17.4 us
    ppermute x1, waiting for transfers between devices: 9.46 us -> 6.51 us  [local(): lax.ppermute(sent, 'basis', along([(1, 3), (2, 0), (0, 1), (3, 2)]))]
    unnamed x1 -> x5, local copies, waits for them, and re-layouts: 0.77 us -> 3.34 us
    ppermute x1, starting transfers between devices: 1.32 us -> 3.63 us  [local(): relayed = lax.ppermute(sent, 'basis', along([(0, 1), (3, 2)]))]
    ppermute x1, starting transfers between devices: 2.07 us -> 0.65 us  [local(): lax.ppermute(sent, 'basis', along([(1, 3), (2, 0), (0, 1), (3, 2)]))]
    ppermute x10, waiting for transfers between devices: 13.8 us -> 12.9 us  [exchange(): return lax.ppermute(array, axis, [(i, i ^ bit) for i in range(peers)])]
    ppermute x10, starting transfers between devices: 5.43 us -> 6.36 us  [exchange(): return lax.ppermute(array, axis, [(i, i ^ bit) for i in range(peers)])]
  transfers between devices with their start and end apart: 15 -> 15, of which waited for: 9 -> 8; matrix products, arithmetic and copies ran while one was open for 3% -> 3% of each run, Pallas kernels for 41% -> 41%
where the time goes in v2:
time: 91 us; the launch traced here: 90.6 us
  Pallas kernels  46.6 us (51%)
  waiting for transfers between devices  19.4 us (21%)
  starting transfers between devices  17.4 us (19%)
  local copies, waits for them, and re-layouts  4.18 us (5%)
  other arithmetic  2.19 us (2%)
    pallas_call x10, Pallas kernels, product(): pl.pallas_call(functools.partial(product_kernel, step, kept, following, l...  37.3 us
    ppermute x10, waiting for transfers between devices, exchange(): return lax.ppermute(array, axis, [(i, i ^ bit) for i in range(peers)])  12.9 us
    pallas_call x1, Pallas kernels, half_rows(): pl.pallas_call(functools.partial(half_kernel, groups, blocks, following),...  7.05 us
    ppermute x1, waiting for transfers between devices, local(): lax.ppermute(sent, 'basis', along([(1, 3), (2, 0), (0, 1), (3, 2)]))  6.51 us
    ppermute x10, starting transfers between devices, exchange(): return lax.ppermute(array, axis, [(i, i ^ bit) for i in range(peers)])  6.36 us
    ppermute x1, starting transfers between devices, local(): after = lax.ppermute(jnp.where(even, first, last), 'basis', ring)  6 us
    ppermute x1, starting transfers between devices, local(): relayed = lax.ppermute(sent, 'basis', along([(0, 1), (3, 2)]))  3.63 us
    unnamed x5, local copies, waits for them, and re-layouts  3.34 us
  transfers between devices with their start and end apart: 15, of which 8 were waited for; matrix products, arithmetic and copies ran while one was open for 3% of the time, Pallas kernels for 41%

profile of v2, /device:TPU:0, one launch (start us, length us, event | category | flops | bytes accessed | tf_op | source)
XLA Modules:
  0.0 90.6 jit_solution(1445405304941979248)
XLA Ops:
  0.0 0.7 broadcast_select_fusion
  0.7 6.0 %collective-permute-start.1 = (bf16[8,1024]{1,0:T(8,128)(2,1)S(1)}, bf16[8,1024]{1,0:T(8,128)(2,1)S(1)}, u32[]{:S(2)}, u32[]{:S(2)}) collective-permute-start(bf16[8,1024]{1,0:T(8,128)(2,1)S(1)} %get-tuple-element.51), channel_id=1, source_target_pairs={{0,7},{1,2},{2,1},{3,4},{4,3},{5,6},{6,5},{7,0},{8,15},{9,10},{10,... | collective-permute-start | bytes 49160 | tf_op jit(solution)/shard_map/ppermute | solution.py:237
  6.7 0.0 collective-permute-start
  7.4 0.8 copy.6.map_ref
  8.2 0.8 pad.4.table_ref
  9.0 0.0 collective-permute-done.1.next_ref
  9.0 1.5 %collective-permute-done.pair_ref = bf16[8,1024]{1,0:T(8,128)(2,1)S(1)} collective-permute-done((bf16[8,1024]{1,0:T(8,128)(2,1)S(1)}, bf16[8,1024]{1,0:T(8,128)(2,1)S(1)}, u32[]{:S(2)}, u32[]{:S(2)}) %collective-permute-start) | collective-permute-done | bytes 16416 | tf_op jit(solution)/shard_map/ppermute | solution.py:23
  10.5 7.0 %shard_map.55 = (bf16[64,3840]{1,0:T(8,128)(2,1)S(1)}, bf16[768,1024]{1,0:T(8,128)(2,1)S(1)}) custom-call(s32[1]{0:T(128)} %bitcast.1.basis_ref, s32[1,48,2]{2,1,0:T(8,128)S(1)} %copy.6.map_ref, s32[1,1]{1,0:T(1,128)S(6)} %copy.7.count_ref, bf16[8,5888]{1,0:T(8,128)(2,1)S(1)} %pad.4.table_ref, bf16[8,1024]{1,0:T(8,128)(2,1)S(1)} %collective-permute-done.pair_ref, ...), custom_call_target="tpu_custom_call" | custom-call | flops 100663296 | bytes 12582912 | tf_op jit(solution)/shard_map/pallas_call | solution.py:96
  17.5 0.1 collective-permute-start.2
  17.6 1.6 %collective-permute-start.3 = (bf16[64,3840]{1,0:T(8,128)(2,1)S(1)}, bf16[64,3840]{1,0:T(8,128)(2,1)S(1)}, u32[]{:S(2)}, u32[]{:S(2)}) collective-permute-start(bf16[64,3840]{1,0:T(8,128)(2,1)S(1)} %get-tuple-element.29.refs_0_), channel_id=1, source_target_pairs={{0,16},{8,24},{16,0},{24,8},{1,17},{9,25},{17,1},{25,9},{2,18},{10... | collective-permute-start | bytes 1474568 | tf_op jit(solution)/shard_map/ppermute | solution.py:23
  19.2 0.3 collective-permute-done.2.refs_1_
  19.5 3.4 %shard_map.56 = (bf16[128,1024]{1,0:T(8,128)(2,1)S(1)}, bf16[768,1024]{1,0:T(8,128)(2,1)S(1)}) custom-call(s32[1]{0:T(128)} %bitcast.1.basis_ref, bf16[3840,8192]{1,0:T(8,128)(2,1)} %virt_ref.21, bf16[768,1024]{1,0:T(8,128)(2,1)S(1)} %get-tuple-element.28.first_ref, bf16[64,3840]{1,0:T(8,128)(2,1)S(1)} %get-tuple-element.29.refs_0_, ...), custom_call_target="tpu_custom_call" | custom-call | flops 1006632960 | bytes 7864320 | tf_op jit(solution)/shard_map/pallas_call | solution.py:181
  22.9 0.6 collective-permute-start.4
  23.5 3.4 %shard_map.57 = (bf16[128,1024]{1,0:T(8,128)(2,1)S(1)}, bf16[768,1024]{1,0:T(8,128)(2,1)S(1)}) custom-call(s32[1]{0:T(128)} %bitcast.1.basis_ref, bf16[3840,8192]{1,0:T(8,128)(2,1)} %virt_ref.21, bf16[768,1024]{1,0:T(8,128)(2,1)S(1)} %get-tuple-element.30.first_ref, bf16[64,3840]{1,0:T(8,128)(2,1)S(1)} %get-tuple-element.29.refs_0_, ...), custom_call_target="tpu_custom_call" | custom-call | flops 1006632960 | bytes 7864320 | tf_op jit(solution)/shard_map/pallas_call | solution.py:181
  26.9 4.4 %collective-permute-done.3.refs_0_.refs_2_ = bf16[64,3840]{1,0:T(8,128)(2,1)S(1)} collective-permute-done((bf16[64,3840]{1,0:T(8,128)(2,1)S(1)}, bf16[64,3840]{1,0:T(8,128)(2,1)S(1)}, u32[]{:S(2)}, u32[]{:S(2)}) %collective-permute-start.3) | collective-permute-done | bytes 491552 | tf_op jit(solution)/shard_map/ppermute | solution.py:23
  31.3 0.0 collective-permute-done.4.refs_4_
  31.3 0.0 collective-permute-start.5
  31.3 0.6 collective-permute-start.6
  31.9 1.3 %collective-permute-done.5.refs_1_.refs_3_ = bf16[64,3840]{1,0:T(8,128)(2,1)S(1)} collective-permute-done((bf16[64,3840]{1,0:T(8,128)(2,1)S(1)}, bf16[64,3840]{1,0:T(8,128)(2,1)S(1)}, u32[]{:S(2)}, u32[]{:S(2)}) %collective-permute-start.5) | collective-permute-done | bytes 491552 | tf_op jit(solution)/shard_map/ppermute | solution.py:23
  33.2 3.4 %shard_map.58 = (bf16[128,1024]{1,0:T(8,128)(2,1)S(1)}, bf16[768,1024]{1,0:T(8,128)(2,1)S(1)}) custom-call(s32[1]{0:T(128)} %bitcast.1.basis_ref, bf16[3840,8192]{1,0:T(8,128)(2,1)} %virt_ref.21, bf16[768,1024]{1,0:T(8,128)(2,1)S(1)} %get-tuple-element.31.first_ref, bf16[64,3840]{1,0:T(8,128)(2,1)S(1)} %collective-permute-done.3.refs_0_.refs_2_, ...), custom_call_target="tpu_custom_call" | custom-call | flops 1006632960 | bytes 7864320 | tf_op jit(solution)/shard_map/pallas_call | solution.py:181
  36.6 0.6 collective-permute-start.7
  37.2 3.2 %collective-permute-done.6.refs_4_ = bf16[128,1024]{1,0:T(8,128)(2,1)S(1)} collective-permute-done((bf16[128,1024]{1,0:T(8,128)(2,1)S(1)}, bf16[128,1024]{1,0:T(8,128)(2,1)S(1)}, u32[]{:S(2)}, u32[]{:S(2)}) %collective-permute-start.6) | collective-permute-done | bytes 262176 | tf_op jit(solution)/shard_map/ppermute | solution.py:23
  40.4 3.8 %shard_map.59 = (bf16[256,1024]{1,0:T(8,128)(2,1)S(1)}, bf16[768,1024]{1,0:T(8,128)(2,1)S(1)}) custom-call(s32[1]{0:T(128)} %bitcast.1.basis_ref, bf16[3840,8192]{1,0:T(8,128)(2,1)} %virt_ref.21, bf16[768,1024]{1,0:T(8,128)(2,1)S(1)} %get-tuple-element.34.first_ref, bf16[64,3840]{1,0:T(8,128)(2,1)S(1)} %get-tuple-element.29.refs_0_, ...), custom_call_target="tpu_custom_call" | custom-call | flops 2013265920 | bytes 7864320 | tf_op jit(solution)/shard_map/pallas_call | solution.py:181
  44.2 0.6 collective-permute-start.8
  44.9 0.8 collective-permute-done.7.refs_5_
  45.6 3.6 %shard_map.60 = (bf16[256,1024]{1,0:T(8,128)(2,1)S(1)}, bf16[768,1024]{1,0:T(8,128)(2,1)S(1)}) custom-call(s32[1]{0:T(128)} %bitcast.1.basis_ref, bf16[3840,8192]{1,0:T(8,128)(2,1)} %virt_ref.21, bf16[768,1024]{1,0:T(8,128)(2,1)S(1)} %get-tuple-element.36.first_ref, bf16[64,3840]{1,0:T(8,128)(2,1)S(1)} %get-tuple-element.29.refs_0_, ...), custom_call_target="tpu_custom_call" | custom-call | flops 2013265920 | bytes 7864320 | tf_op jit(solution)/shard_map/pallas_call | solution.py:181
  49.2 0.7 collective-permute-start.10
  49.9 3.6 %collective-permute-start.11 = (bf16[256,1024]{1,0:T(8,128)(2,1)S(1)}, bf16[256,1024]{1,0:T(8,128)(2,1)S(1)}, u32[]{:S(2)}, u32[]{:S(2)}) collective-permute-start(bf16[256,1024]{1,0:T(8,128)(2,1)S(1)} %get-tuple-element.43), channel_id=1, source_target_pairs={{0,2},{1,3},{6,4},{7,5},{8,10},{9,11},{14,12},{15,13},{16,18},{17,... | collective-permute-start | bytes 1572872 | tf_op jit(solution)/shard_map/ppermute | solution.py:283
  53.6 3.4 %shard_map.61 = (bf16[128,1024]{1,0:T(8,128)(2,1)S(1)}, bf16[768,1024]{1,0:T(8,128)(2,1)S(1)}) custom-call(s32[1]{0:T(128)} %bitcast.1.basis_ref, bf16[3840,8192]{1,0:T(8,128)(2,1)} %virt_ref.21, bf16[768,1024]{1,0:T(8,128)(2,1)S(1)} %get-tuple-element.38.first_ref, bf16[64,3840]{1,0:T(8,128)(2,1)S(1)} %collective-permute-done.3.refs_0_.refs_2_, ...), custom_call_target="tpu_custom_call" | custom-call | flops 1006632960 | bytes 7864320 | tf_op jit(solution)/shard_map/pallas_call | solution.py:181
  57.0 1.4 %collective-permute-start.9 = (bf16[128,1024]{1,0:T(8,128)(2,1)S(1)}, bf16[128,1024]{1,0:T(8,128)(2,1)S(1)}, u32[]{:S(2)}, u32[]{:S(2)}) collective-permute-start(bf16[128,1024]{1,0:T(8,128)(2,1)S(1)} %get-tuple-element.42), channel_id=1, source_target_pairs={{0,1},{1,0},{2,3},{3,2},{4,5},{5,4},{6,7},{7,6},{8,9},{9,8},{10,11... | collective-permute-start | bytes 786440 | tf_op jit(solution)/shard_map/ppermute | solution.py:23
  58.4 0.0 collective-permute-done.8.refs_4_
  58.4 4.4 %shard_map.62 = (bf16[256,1024]{1,0:T(8,128)(2,1)}, bf16[768,1024]{1,0:T(8,128)(2,1)S(1)}) custom-call(s32[1]{0:T(128)} %bitcast.1.basis_ref, bf16[3840,8192]{1,0:T(8,128)(2,1)} %virt_ref.21, bf16[768,1024]{1,0:T(8,128)(2,1)S(1)} %get-tuple-element.39.first_ref, bf16[64,3840]{1,0:T(8,128)(2,1)S(1)} %get-tuple-element.29.refs_0_, ...), custom_call_target="tpu_custom_call" | custom-call | flops 2013265920 | bytes 7864320 | tf_op jit(solution)/shard_map/pallas_call | solution.py:181
  62.8 0.1 collective-permute-start.12
  62.9 1.4 %collective-permute-done.9.refs_5_ = bf16[128,1024]{1,0:T(8,128)(2,1)S(1)} collective-permute-done((bf16[128,1024]{1,0:T(8,128)(2,1)S(1)}, bf16[128,1024]{1,0:T(8,128)(2,1)S(1)}, u32[]{:S(2)}, u32[]{:S(2)}) %collective-permute-start.9) | collective-permute-done | bytes 262176 | tf_op jit(solution)/shard_map/ppermute | solution.py:23
  64.3 0.0 collective-permute-done.10.refs_6_
  64.3 3.8 %shard_map.63 = (f32[256,1024]{1,0:T(8,128)S(1)}, bf16[768,1024]{1,0:T(8,128)(2,1)S(1)}) custom-call(s32[1]{0:T(128)} %bitcast.1.basis_ref, bf16[3840,8192]{1,0:T(8,128)(2,1)} %virt_ref.21, bf16[768,1024]{1,0:T(8,128)(2,1)S(1)} %get-tuple-element.41.first_ref, bf16[64,3840]{1,0:T(8,128)(2,1)S(1)} %get-tuple-element.29.refs_0_, ...), custom_call_target="tpu_custom_call" | custom-call | flops 2013265920 | bytes 7864320 | tf_op jit(solution)/shard_map/pallas_call | solution.py:181
  68.1 0.0 collective-permute-done.11
  68.2 0.2 add_convert_fusion.refs_4_
  68.3 0.6 collective-permute-start.13
  69.0 4.4 %shard_map.64 = (bf16[256,1024]{1,0:T(8,128)(2,1)}, bf16[768,1024]{1,0:T(8,128)(2,1)S(1)}) custom-call(s32[1]{0:T(128)} %bitcast.1.basis_ref, bf16[3840,8192]{1,0:T(8,128)(2,1)} %virt_ref.21, bf16[768,1024]{1,0:T(8,128)(2,1)S(1)} %get-tuple-element.44.first_ref, bf16[64,3840]{1,0:T(8,128)(2,1)S(1)} %get-tuple-element.29.refs_0_, ...), custom_call_target="tpu_custom_call" | custom-call | flops 2013265920 | bytes 7864320 | tf_op jit(solution)/shard_map/pallas_call | solution.py:181
  73.4 0.0 copy-start
  73.4 1.2 %copy-done = bf16[768,1024]{1,0:T(8,128)(2,1)} copy-done((bf16[768,1024]{1,0:T(8,128)(2,1)}, bf16[768,1024]{1,0:T(8,128)(2,1)S(1)}, u32[]{:S(2)}) %copy-start) | copy-done | bytes 1572888
  74.6 0.9 collective-permute-start.14
  75.5 0.0 copy-start.1
  75.5 1.4 %copy-done.1 = bf16[768,1024]{1,0:T(8,128)(2,1)S(1)} copy-done((bf16[768,1024]{1,0:T(8,128)(2,1)S(1)}, bf16[768,1024]{1,0:T(8,128)(2,1)}, u32[]{:S(2)}) %copy-start.1) | copy-done | bytes 1572888
  76.9 3.6 %shard_map.65 = f32[256,1024]{1,0:T(8,128)S(1)} custom-call(s32[1]{0:T(128)} %bitcast.1.basis_ref, bf16[3840,8192]{1,0:T(8,128)(2,1)} %virt_ref.21, bf16[768,1024]{1,0:T(8,128)(2,1)S(1)} %copy-done.1, bf16[64,3840]{1,0:T(8,128)(2,1)S(1)} %get-tuple-element.29.refs_0_, bf16[64,3840]{1,0:T(8,128)(2,1)S(1)} %collective-permute-done.2.refs_1_, ...), custom_call_target="tpu_custom_call" | custom-call | flops 2013265920 | bytes 7864320 | tf_op jit(solution)/shard_map/pallas_call | solution.py:181
  80.5 0.0 collective-permute-done.12
  80.5 1.3 %convert_add_fusion.total_ref = f32[256,1024]{1,0:T(8,128)S(1)} fusion(bf16[256,1024]{1,0:T(8,128)(2,1)} %collective-permute-done.12, f32[256,1024]{1,0:T(8,128)S(1)} %shard_map.65, bf16[256,1024]{1,0:T(8,128)(2,1)S(1)} %collective-permute-done.10.refs_6_), kind=kLoop, calls=%fused_computation | loop fusion | flops 1048576 | bytes 3145728 | tf_op jit(solution)/shard_map/add | solution.py:293
  81.8 6.5 %collective-permute-done.13.refs_1_ = bf16[256,1024]{1,0:T(8,128)(2,1)S(1)} collective-permute-done((bf16[256,1024]{1,0:T(8,128)(2,1)S(1)}, bf16[256,1024]{1,0:T(8,128)(2,1)S(1)}, u32[]{:S(2)}, u32[]{:S(2)}) %collective-permute-start.13) | collective-permute-done | bytes 524320 | tf_op jit(solution)/shard_map/ppermute | solution.py:290
  88.3 0.0 collective-permute-done.14.refs_0_
  88.3 2.3 %shard_map.66 = bf16[1024,256]{1,0:T(8,128)(2,1)} custom-call(s32[1]{0:T(128)} %bitcast.aux_ref, f32[256,1024]{1,0:T(8,128)S(1)} %convert_add_fusion.total_ref, bf16[256,1024]{1,0:T(8,128)(2,1)} %collective-permute-done.14.refs_0_, bf16[256,1024]{1,0:T(8,128)(2,1)S(1)} %collective-permute-done.13.refs_1_), custom_call_target="tpu_custom_call" | custom-call | tf_op jit(solution)/shard_map/pallas_call | solution.py:215
Async XLA Ops:
  0.7 8.3 %collective-permute-start.1 = (bf16[8,1024]{1,0:T(8,128)(2,1)S(1)}, bf16[8,1024]{1,0:T(8,128)(2,1)S(1)}, u32[]{:S(2)}, u32[]{:S(2)}) collective-permute-start(bf16[8,1024]{1,0:T(8,128)(2,1)S(1)} %get-tuple-element.51), channel_id=1, source_target_pairs={{0,7},{1,2},{2,1},{3,4},{4,3},{5,6},{6,5},{7,0},{8,15},{9,10},{10,... | collective-permute-start | bytes 49160 | tf_op jit(solution)/shard_map/ppermute | solution.py:237
  6.7 3.7 %collective-permute-start = (bf16[8,1024]{1,0:T(8,128)(2,1)S(1)}, bf16[8,1024]{1,0:T(8,128)(2,1)S(1)}, u32[]{:S(2)}, u32[]{:S(2)}) collective-permute-start(bf16[8,1024]{1,0:T(8,128)(2,1)S(1)} %get-tuple-element.52), channel_id=1, source_target_pairs={{0,1},{1,0},{2,3},{3,2},{4,5},{5,4},{6,7},{7,6},{8,9},{9,8},{10,11... | collective-permute-start | bytes 49160 | tf_op jit(solution)/shard_map/ppermute | solution.py:23
  17.5 1.9 %collective-permute-start.2 = (bf16[64,3840]{1,0:T(8,128)(2,1)S(1)}, bf16[64,3840]{1,0:T(8,128)(2,1)S(1)}, u32[]{:S(2)}, u32[]{:S(2)}) collective-permute-start(bf16[64,3840]{1,0:T(8,128)(2,1)S(1)} %get-tuple-element.29.refs_0_), channel_id=1, source_target_pairs={{0,8},{8,0},{16,24},{24,16},{1,9},{9,1},{17,25},{25,17},{2,10},{10... | collective-permute-start | bytes 1474568 | tf_op jit(solution)/shard_map/ppermute | solution.py:23
  17.6 13.6 %collective-permute-start.3 = (bf16[64,3840]{1,0:T(8,128)(2,1)S(1)}, bf16[64,3840]{1,0:T(8,128)(2,1)S(1)}, u32[]{:S(2)}, u32[]{:S(2)}) collective-permute-start(bf16[64,3840]{1,0:T(8,128)(2,1)S(1)} %get-tuple-element.29.refs_0_), channel_id=1, source_target_pairs={{0,16},{8,24},{16,0},{24,8},{1,17},{9,25},{17,1},{25,9},{2,18},{10... | collective-permute-start | bytes 1474568 | tf_op jit(solution)/shard_map/ppermute | solution.py:23
  22.9 8.4 %collective-permute-start.4 = (bf16[128,1024]{1,0:T(8,128)(2,1)S(1)}, bf16[128,1024]{1,0:T(8,128)(2,1)S(1)}, u32[]{:S(2)}, u32[]{:S(2)}) collective-permute-start(bf16[128,1024]{1,0:T(8,128)(2,1)S(1)} %get-tuple-element.32), channel_id=1, source_target_pairs={{0,1},{1,0},{2,3},{3,2},{4,5},{5,4},{6,7},{7,6},{8,9},{9,8},{10,11... | collective-permute-start | bytes 786440 | tf_op jit(solution)/shard_map/ppermute | solution.py:23
  31.3 1.9 %collective-permute-start.5 = (bf16[64,3840]{1,0:T(8,128)(2,1)S(1)}, bf16[64,3840]{1,0:T(8,128)(2,1)S(1)}, u32[]{:S(2)}, u32[]{:S(2)}) collective-permute-start(bf16[64,3840]{1,0:T(8,128)(2,1)S(1)} %collective-permute-done.3.refs_0_.refs_2_), channel_id=1, source_target_pairs={{0,8},{8,0},{16,24},{24,16},{1,9},{9,1},{17,25},{25,17},{2,10},{10... | collective-permute-start | bytes 1474568 | tf_op jit(solution)/shard_map/ppermute | solution.py:23
  31.3 9.1 %collective-permute-start.6 = (bf16[128,1024]{1,0:T(8,128)(2,1)S(1)}, bf16[128,1024]{1,0:T(8,128)(2,1)S(1)}, u32[]{:S(2)}, u32[]{:S(2)}) collective-permute-start(bf16[128,1024]{1,0:T(8,128)(2,1)S(1)} %get-tuple-element.35), channel_id=1, source_target_pairs={{0,1},{1,0},{2,3},{3,2},{4,5},{5,4},{6,7},{7,6},{8,9},{9,8},{10,11... | collective-permute-start | bytes 786440 | tf_op jit(solution)/shard_map/ppermute | solution.py:23
  36.6 9.1 %collective-permute-start.7 = (bf16[128,1024]{1,0:T(8,128)(2,1)S(1)}, bf16[128,1024]{1,0:T(8,128)(2,1)S(1)}, u32[]{:S(2)}, u32[]{:S(2)}) collective-permute-start(bf16[128,1024]{1,0:T(8,128)(2,1)S(1)} %get-tuple-element.37), channel_id=1, source_target_pairs={{0,1},{1,0},{2,3},{3,2},{4,5},{5,4},{6,7},{7,6},{8,9},{9,8},{10,11... | collective-permute-start | bytes 786440 | tf_op jit(solution)/shard_map/ppermute | solution.py:23
  44.2 14.2 %collective-permute-start.8 = (bf16[256,1024]{1,0:T(8,128)(2,1)S(1)}, bf16[256,1024]{1,0:T(8,128)(2,1)S(1)}, u32[]{:S(2)}, u32[]{:S(2)}) collective-permute-start(bf16[256,1024]{1,0:T(8,128)(2,1)S(1)} %get-tuple-element.40), channel_id=1, source_target_pairs={{0,1},{1,0},{2,3},{3,2},{4,5},{5,4},{6,7},{7,6},{8,9},{9,8},{10,11... | collective-permute-start | bytes 1572872 | tf_op jit(solution)/shard_map/ppermute | solution.py:23
  49.2 15.1 %collective-permute-start.10 = (bf16[256,1024]{1,0:T(8,128)(2,1)S(1)}, bf16[256,1024]{1,0:T(8,128)(2,1)S(1)}, u32[]{:S(2)}, u32[]{:S(2)}) collective-permute-start(bf16[256,1024]{1,0:T(8,128)(2,1)S(1)} %get-tuple-element.43), channel_id=1, source_target_pairs={{2,4},{3,5},{4,2},{5,3},{10,12},{11,13},{12,10},{13,11},{18,20},{1... | collective-permute-start | bytes 1572872 | tf_op jit(solution)/shard_map/ppermute | solution.py:284
  49.9 18.2 %collective-permute-start.11 = (bf16[256,1024]{1,0:T(8,128)(2,1)S(1)}, bf16[256,1024]{1,0:T(8,128)(2,1)S(1)}, u32[]{:S(2)}, u32[]{:S(2)}) collective-permute-start(bf16[256,1024]{1,0:T(8,128)(2,1)S(1)} %get-tuple-element.43), channel_id=1, source_target_pairs={{0,2},{1,3},{6,4},{7,5},{8,10},{9,11},{14,12},{15,13},{16,18},{17,... | collective-permute-start | bytes 1572872 | tf_op jit(solution)/shard_map/ppermute | solution.py:283
  57.0 7.3 %collective-permute-start.9 = (bf16[128,1024]{1,0:T(8,128)(2,1)S(1)}, bf16[128,1024]{1,0:T(8,128)(2,1)S(1)}, u32[]{:S(2)}, u32[]{:S(2)}) collective-permute-start(bf16[128,1024]{1,0:T(8,128)(2,1)S(1)} %get-tuple-element.42), channel_id=1, source_target_pairs={{0,1},{1,0},{2,3},{3,2},{4,5},{5,4},{6,7},{7,6},{8,9},{9,8},{10,11... | collective-permute-start | bytes 786440 | tf_op jit(solution)/shard_map/ppermute | solution.py:23
  62.8 17.7 %collective-permute-start.12 = (bf16[256,1024]{1,0:T(8,128)(2,1)}, bf16[256,1024]{1,0:T(8,128)(2,1)}, u32[]{:S(2)}, u32[]{:S(2)}) collective-permute-start(bf16[256,1024]{1,0:T(8,128)(2,1)} %get-tuple-element.47), channel_id=1, source_target_pairs={{0,4},{1,5},{6,2},{7,3},{2,0},{3,1},{4,6},{5,7},{8,12},{9,13},{14,... | collective-permute-start | bytes 1572872 | tf_op jit(solution)/shard_map/ppermute | solution.py:287
  68.3 20.0 %collective-permute-start.13 = (bf16[256,1024]{1,0:T(8,128)(2,1)S(1)}, bf16[256,1024]{1,0:T(8,128)(2,1)S(1)}, u32[]{:S(2)}, u32[]{:S(2)}) collective-permute-start(bf16[256,1024]{1,0:T(8,128)(2,1)S(1)} %add_convert_fusion.refs_4_), channel_id=1, source_target_pairs={{2,6},{3,7},{4,0},{5,1},{0,2},{1,3},{6,4},{7,5},{10,14},{11,15},{1... | collective-permute-start | bytes 1572872 | tf_op jit(solution)/shard_map/ppermute | solution.py:290
  73.4 1.2 %copy-start = (bf16[768,1024]{1,0:T(8,128)(2,1)}, bf16[768,1024]{1,0:T(8,128)(2,1)S(1)}, u32[]{:S(2)}) copy-start(bf16[768,1024]{1,0:T(8,128)(2,1)S(1)} %get-tuple-element.46.first_ref) | copy-start | bytes 4718596
  74.6 13.7 %collective-permute-start.14 = (bf16[256,1024]{1,0:T(8,128)(2,1)}, bf16[256,1024]{1,0:T(8,128)(2,1)}, u32[]{:S(2)}, u32[]{:S(2)}) collective-permute-start(bf16[256,1024]{1,0:T(8,128)(2,1)} %get-tuple-element.49), channel_id=1, source_target_pairs={{0,1},{1,0},{2,3},{3,2},{4,5},{5,4},{6,7},{7,6},{8,9},{9,8},{10,11... | collective-permute-start | bytes 1572872 | tf_op jit(solution)/shard_map/ppermute | solution.py:23
  75.5 1.4 %copy-start.1 = (bf16[768,1024]{1,0:T(8,128)(2,1)S(1)}, bf16[768,1024]{1,0:T(8,128)(2,1)}, u32[]{:S(2)}) copy-start(bf16[768,1024]{1,0:T(8,128)(2,1)} %copy-done) | copy-start | bytes 4718596

commit v3 on v2

--- a/solution.py
+++ b/solution.py
@@ -280,12 +280,12 @@
     if groups == 4:
         sent = mult(3, True, every, (received[3],))
         along = lambda pairs: [(2 * a + s, 2 * b + s) for a, b in pairs for s in (0, 1)]
+        inner = lax.ppermute(sent, "basis", along([(1, 2), (2, 1)]))
         relayed = lax.ppermute(sent, "basis", along([(0, 1), (3, 2)]))
-        inner = lax.ppermute(sent, "basis", along([(1, 2), (2, 1)]))
         received[THIRD] += (send(THIRD, late),)
         sent = mult(SECOND, True, every, (received[SECOND],))
         third = lax.ppermute(sent, "basis", along([(0, 2), (3, 1), (1, 0), (2, 3)]))
-        part = mult(THIRD, True, every, (received[THIRD],), after=(inner,), dtype=F32)
+        part = mult(THIRD, True, every, (received[THIRD],), after=(inner, relayed), dtype=F32)
         sent = (part + relayed.astype(F32)).astype(BF16)
         fourth = lax.ppermute(sent, "basis", along([(1, 3), (2, 0), (0, 1), (3, 2)]))
         received[0] = (send(0, every, after=(sent,)),)

time: 91 us -> 97.1 us (1.067)
  starting transfers between devices: 17.4 us -> 27.4 us
  waiting for transfers between devices: 19.4 us -> 15.6 us
    ppermute x1, starting transfers between devices: 0.65 us -> 10.5 us  [local(): lax.ppermute(sent, 'basis', along([(1, 3), (2, 0), (0, 1), (3, 2)]))]
    ppermute x1, waiting for transfers between devices: 6.51 us -> 0.01 us  [local(): lax.ppermute(sent, 'basis', along([(1, 3), (2, 0), (0, 1), (3, 2)]))]
    ppermute x10, waiting for transfers between devices: 12.9 us -> 15.6 us  [exchange(): return lax.ppermute(array, axis, [(i, i ^ bit) for i in range(peers)])]
    ppermute x1, starting transfers between devices: 3.63 us -> 1.32 us  [local(): relayed = lax.ppermute(sent, 'basis', along([(0, 1), (3, 2)]))]
    ppermute x10, starting transfers between devices: 6.36 us -> 8.63 us  [exchange(): return lax.ppermute(array, axis, [(i, i ^ bit) for i in range(peers)])]
  transfers between devices with their start and end apart: 15 -> 15, of which waited for: 8 -> 9; matrix products, arithmetic and copies ran while one was open for 3% -> 3% of each run, Pallas kernels for 41% -> 39%
where the time goes in v3:
time: 97.1 us; the launch traced here: 96.7 us
  Pallas kernels  46.6 us (48%)
  starting transfers between devices  27.4 us (28%)
  waiting for transfers between devices  15.6 us (16%)
  local copies, waits for them, and re-layouts  4.18 us (4%)
  other arithmetic  2.19 us (2%)
    pallas_call x10, Pallas kernels, product(): pl.pallas_call(functools.partial(product_kernel, step, kept, following, l...  37.3 us
    ppermute x10, waiting for transfers between devices, exchange(): return lax.ppermute(array, axis, [(i, i ^ bit) for i in range(peers)])  15.6 us
    ppermute x1, starting transfers between devices, local(): lax.ppermute(sent, 'basis', along([(1, 3), (2, 0), (0, 1), (3, 2)]))  10.5 us
    ppermute x10, starting transfers between devices, exchange(): return lax.ppermute(array, axis, [(i, i ^ bit) for i in range(peers)])  8.63 us
    pallas_call x1, Pallas kernels, half_rows(): pl.pallas_call(functools.partial(half_kernel, groups, blocks, following),...  7.04 us
    ppermute x1, starting transfers between devices, local(): after = lax.ppermute(jnp.where(even, first, last), 'basis', ring)  6 us
    unnamed x5, local copies, waits for them, and re-layouts  3.34 us
    pallas_call x1, Pallas kernels, finish(): pl.pallas_call(functools.partial(finish_kernel, slab, tuple((len(add) for...  2.27 us
  transfers between devices with their start and end apart: 15, of which 9 were waited for; matrix products, arithmetic and copies ran while one was open for 3% of the time, Pallas kernels for 39%

profile of v3, /device:TPU:0, one launch (start us, length us, event | category | flops | bytes accessed | tf_op | source)
XLA Modules:
  0.0 96.7 jit_solution(3312397321045764994)
XLA Ops:
  0.0 0.7 broadcast_select_fusion
  0.7 6.0 %collective-permute-start.1 = (bf16[8,1024]{1,0:T(8,128)(2,1)S(1)}, bf16[8,1024]{1,0:T(8,128)(2,1)S(1)}, u32[]{:S(2)}, u32[]{:S(2)}) collective-permute-start(bf16[8,1024]{1,0:T(8,128)(2,1)S(1)} %get-tuple-element.51), channel_id=1, source_target_pairs={{0,7},{1,2},{2,1},{3,4},{4,3},{5,6},{6,5},{7,0},{8,15},{9,10},{10,... | collective-permute-start | bytes 49160 | tf_op jit(solution)/shard_map/ppermute | solution.py:237
  6.7 0.0 collective-permute-start
  7.4 0.8 copy.6.map_ref
  8.2 0.8 pad.4.table_ref
  9.0 0.0 collective-permute-done.1.next_ref
  9.0 1.5 %collective-permute-done.pair_ref = bf16[8,1024]{1,0:T(8,128)(2,1)S(1)} collective-permute-done((bf16[8,1024]{1,0:T(8,128)(2,1)S(1)}, bf16[8,1024]{1,0:T(8,128)(2,1)S(1)}, u32[]{:S(2)}, u32[]{:S(2)}) %collective-permute-start) | collective-permute-done | bytes 16416 | tf_op jit(solution)/shard_map/ppermute | solution.py:23
  10.5 7.0 %shard_map.55 = (bf16[64,3840]{1,0:T(8,128)(2,1)S(1)}, bf16[768,1024]{1,0:T(8,128)(2,1)S(1)}) custom-call(s32[1]{0:T(128)} %bitcast.1.basis_ref, s32[1,48,2]{2,1,0:T(8,128)S(1)} %copy.6.map_ref, s32[1,1]{1,0:T(1,128)S(6)} %copy.7.count_ref, bf16[8,5888]{1,0:T(8,128)(2,1)S(1)} %pad.4.table_ref, bf16[8,1024]{1,0:T(8,128)(2,1)S(1)} %collective-permute-done.pair_ref, ...), custom_call_target="tpu_custom_call" | custom-call | flops 100663296 | bytes 12582912 | tf_op jit(solution)/shard_map/pallas_call | solution.py:96
  17.5 0.1 collective-permute-start.2
  17.6 1.6 %collective-permute-start.3 = (bf16[64,3840]{1,0:T(8,128)(2,1)S(1)}, bf16[64,3840]{1,0:T(8,128)(2,1)S(1)}, u32[]{:S(2)}, u32[]{:S(2)}) collective-permute-start(bf16[64,3840]{1,0:T(8,128)(2,1)S(1)} %get-tuple-element.29.refs_0_), channel_id=1, source_target_pairs={{0,16},{8,24},{16,0},{24,8},{1,17},{9,25},{17,1},{25,9},{2,18},{10... | collective-permute-start | bytes 1474568 | tf_op jit(solution)/shard_map/ppermute | solution.py:23
  19.2 0.3 collective-permute-done.2.refs_1_
  19.5 3.4 %shard_map.56 = (bf16[128,1024]{1,0:T(8,128)(2,1)S(1)}, bf16[768,1024]{1,0:T(8,128)(2,1)S(1)}) custom-call(s32[1]{0:T(128)} %bitcast.1.basis_ref, bf16[3840,8192]{1,0:T(8,128)(2,1)} %virt_ref.21, bf16[768,1024]{1,0:T(8,128)(2,1)S(1)} %get-tuple-element.28.first_ref, bf16[64,3840]{1,0:T(8,128)(2,1)S(1)} %get-tuple-element.29.refs_0_, ...), custom_call_target="tpu_custom_call" | custom-call | flops 1006632960 | bytes 7864320 | tf_op jit(solution)/shard_map/pallas_call | solution.py:181
  22.9 0.6 collective-permute-start.4
  23.5 3.4 %shard_map.57 = (bf16[128,1024]{1,0:T(8,128)(2,1)S(1)}, bf16[768,1024]{1,0:T(8,128)(2,1)S(1)}) custom-call(s32[1]{0:T(128)} %bitcast.1.basis_ref, bf16[3840,8192]{1,0:T(8,128)(2,1)} %virt_ref.21, bf16[768,1024]{1,0:T(8,128)(2,1)S(1)} %get-tuple-element.30.first_ref, bf16[64,3840]{1,0:T(8,128)(2,1)S(1)} %get-tuple-element.29.refs_0_, ...), custom_call_target="tpu_custom_call" | custom-call | flops 1006632960 | bytes 7864320 | tf_op jit(solution)/shard_map/pallas_call | solution.py:181
  26.9 4.4 %collective-permute-done.3.refs_0_.refs_2_ = bf16[64,3840]{1,0:T(8,128)(2,1)S(1)} collective-permute-done((bf16[64,3840]{1,0:T(8,128)(2,1)S(1)}, bf16[64,3840]{1,0:T(8,128)(2,1)S(1)}, u32[]{:S(2)}, u32[]{:S(2)}) %collective-permute-start.3) | collective-permute-done | bytes 491552 | tf_op jit(solution)/shard_map/ppermute | solution.py:23
  31.3 0.0 collective-permute-done.4.refs_4_
  31.3 0.0 collective-permute-start.5
  31.3 0.6 collective-permute-start.6
  31.9 1.3 %collective-permute-done.5.refs_1_.refs_3_ = bf16[64,3840]{1,0:T(8,128)(2,1)S(1)} collective-permute-done((bf16[64,3840]{1,0:T(8,128)(2,1)S(1)}, bf16[64,3840]{1,0:T(8,128)(2,1)S(1)}, u32[]{:S(2)}, u32[]{:S(2)}) %collective-permute-start.5) | collective-permute-done | bytes 491552 | tf_op jit(solution)/shard_map/ppermute | solution.py:23
  33.1 3.4 %shard_map.58 = (bf16[128,1024]{1,0:T(8,128)(2,1)S(1)}, bf16[768,1024]{1,0:T(8,128)(2,1)S(1)}) custom-call(s32[1]{0:T(128)} %bitcast.1.basis_ref, bf16[3840,8192]{1,0:T(8,128)(2,1)} %virt_ref.21, bf16[768,1024]{1,0:T(8,128)(2,1)S(1)} %get-tuple-element.31.first_ref, bf16[64,3840]{1,0:T(8,128)(2,1)S(1)} %collective-permute-done.3.refs_0_.refs_2_, ...), custom_call_target="tpu_custom_call" | custom-call | flops 1006632960 | bytes 7864320 | tf_op jit(solution)/shard_map/pallas_call | solution.py:181
  36.5 0.6 collective-permute-start.7
  37.2 3.2 %collective-permute-done.6.refs_4_ = bf16[128,1024]{1,0:T(8,128)(2,1)S(1)} collective-permute-done((bf16[128,1024]{1,0:T(8,128)(2,1)S(1)}, bf16[128,1024]{1,0:T(8,128)(2,1)S(1)}, u32[]{:S(2)}, u32[]{:S(2)}) %collective-permute-start.6) | collective-permute-done | bytes 262176 | tf_op jit(solution)/shard_map/ppermute | solution.py:23
  40.4 3.8 %shard_map.59 = (bf16[256,1024]{1,0:T(8,128)(2,1)S(1)}, bf16[768,1024]{1,0:T(8,128)(2,1)S(1)}) custom-call(s32[1]{0:T(128)} %bitcast.1.basis_ref, bf16[3840,8192]{1,0:T(8,128)(2,1)} %virt_ref.21, bf16[768,1024]{1,0:T(8,128)(2,1)S(1)} %get-tuple-element.34.first_ref, bf16[64,3840]{1,0:T(8,128)(2,1)S(1)} %get-tuple-element.29.refs_0_, ...), custom_call_target="tpu_custom_call" | custom-call | flops 2013265920 | bytes 7864320 | tf_op jit(solution)/shard_map/pallas_call | solution.py:181
  44.2 0.6 collective-permute-start.8
  44.8 0.8 collective-permute-done.7.refs_5_
  45.6 3.6 %shard_map.60 = (bf16[256,1024]{1,0:T(8,128)(2,1)S(1)}, bf16[768,1024]{1,0:T(8,128)(2,1)S(1)}) custom-call(s32[1]{0:T(128)} %bitcast.1.basis_ref, bf16[3840,8192]{1,0:T(8,128)(2,1)} %virt_ref.21, bf16[768,1024]{1,0:T(8,128)(2,1)S(1)} %get-tuple-element.36.first_ref, bf16[64,3840]{1,0:T(8,128)(2,1)S(1)} %get-tuple-element.29.refs_0_, ...), custom_call_target="tpu_custom_call" | custom-call | flops 2013265920 | bytes 7864320 | tf_op jit(solution)/shard_map/pallas_call | solution.py:181
  49.2 1.3 %collective-permute-start.11 = (bf16[256,1024]{1,0:T(8,128)(2,1)S(1)}, bf16[256,1024]{1,0:T(8,128)(2,1)S(1)}, u32[]{:S(2)}, u32[]{:S(2)}) collective-permute-start(bf16[256,1024]{1,0:T(8,128)(2,1)S(1)} %get-tuple-element.43), channel_id=1, source_target_pairs={{0,2},{1,3},{6,4},{7,5},{8,10},{9,11},{14,12},{15,13},{16,18},{17,... | collective-permute-start | bytes 1572872 | tf_op jit(solution)/shard_map/ppermute | solution.py:284
  50.6 0.9 collective-permute-start.10
  51.4 3.4 %shard_map.61 = (bf16[128,1024]{1,0:T(8,128)(2,1)S(1)}, bf16[768,1024]{1,0:T(8,128)(2,1)S(1)}) custom-call(s32[1]{0:T(128)} %bitcast.1.basis_ref, bf16[3840,8192]{1,0:T(8,128)(2,1)} %virt_ref.21, bf16[768,1024]{1,0:T(8,128)(2,1)S(1)} %get-tuple-element.38.first_ref, bf16[64,3840]{1,0:T(8,128)(2,1)S(1)} %collective-permute-done.3.refs_0_.refs_2_, ...), custom_call_target="tpu_custom_call" | custom-call | flops 1006632960 | bytes 7864320 | tf_op jit(solution)/shard_map/pallas_call | solution.py:181
  54.8 0.8 collective-permute-start.9
  55.6 2.0 %collective-permute-done.8.refs_4_ = bf16[256,1024]{1,0:T(8,128)(2,1)S(1)} collective-permute-done((bf16[256,1024]{1,0:T(8,128)(2,1)S(1)}, bf16[256,1024]{1,0:T(8,128)(2,1)S(1)}, u32[]{:S(2)}, u32[]{:S(2)}) %collective-permute-start.8) | collective-permute-done | bytes 524320 | tf_op jit(solution)/shard_map/ppermute | solution.py:23
  57.6 4.4 %shard_map.62 = (bf16[256,1024]{1,0:T(8,128)(2,1)}, bf16[768,1024]{1,0:T(8,128)(2,1)S(1)}) custom-call(s32[1]{0:T(128)} %bitcast.1.basis_ref, bf16[3840,8192]{1,0:T(8,128)(2,1)} %virt_ref.21, bf16[768,1024]{1,0:T(8,128)(2,1)S(1)} %get-tuple-element.39.first_ref, bf16[64,3840]{1,0:T(8,128)(2,1)S(1)} %get-tuple-element.29.refs_0_, ...), custom_call_target="tpu_custom_call" | custom-call | flops 2013265920 | bytes 7864320 | tf_op jit(solution)/shard_map/pallas_call | solution.py:181
  62.0 0.1 collective-permute-start.12
  62.1 1.0 collective-permute-done.9.refs_5_
  63.1 0.0 collective-permute-done.11.refs_7_
  63.1 0.0 collective-permute-done.10.refs_6_
  63.1 3.8 %shard_map.63 = (f32[256,1024]{1,0:T(8,128)S(1)}, bf16[768,1024]{1,0:T(8,128)(2,1)S(1)}) custom-call(s32[1]{0:T(128)} %bitcast.1.basis_ref, bf16[3840,8192]{1,0:T(8,128)(2,1)} %virt_ref.21, bf16[768,1024]{1,0:T(8,128)(2,1)S(1)} %get-tuple-element.41.first_ref, bf16[64,3840]{1,0:T(8,128)(2,1)S(1)} %get-tuple-element.29.refs_0_, ...), custom_call_target="tpu_custom_call" | custom-call | flops 2013265920 | bytes 7864320 | tf_op jit(solution)/shard_map/pallas_call | solution.py:181
  66.9 0.2 add_convert_fusion.refs_4_
  67.1 10.5 %collective-permute-start.13 = (bf16[256,1024]{1,0:T(8,128)(2,1)S(1)}, bf16[256,1024]{1,0:T(8,128)(2,1)S(1)}, u32[]{:S(2)}, u32[]{:S(2)}) collective-permute-start(bf16[256,1024]{1,0:T(8,128)(2,1)S(1)} %add_convert_fusion.refs_4_), channel_id=1, source_target_pairs={{2,6},{3,7},{4,0},{5,1},{0,2},{1,3},{6,4},{7,5},{10,14},{11,15},{1... | collective-permute-start | bytes 1572872 | tf_op jit(solution)/shard_map/ppermute | solution.py:290
  77.6 4.4 %shard_map.64 = (bf16[256,1024]{1,0:T(8,128)(2,1)}, bf16[768,1024]{1,0:T(8,128)(2,1)S(1)}) custom-call(s32[1]{0:T(128)} %bitcast.1.basis_ref, bf16[3840,8192]{1,0:T(8,128)(2,1)} %virt_ref.21, bf16[768,1024]{1,0:T(8,128)(2,1)S(1)} %get-tuple-element.44.first_ref, bf16[64,3840]{1,0:T(8,128)(2,1)S(1)} %get-tuple-element.29.refs_0_, ...), custom_call_target="tpu_custom_call" | custom-call | flops 2013265920 | bytes 7864320 | tf_op jit(solution)/shard_map/pallas_call | solution.py:181
  82.0 0.0 copy-start
  82.0 1.2 %copy-done = bf16[768,1024]{1,0:T(8,128)(2,1)} copy-done((bf16[768,1024]{1,0:T(8,128)(2,1)}, bf16[768,1024]{1,0:T(8,128)(2,1)S(1)}, u32[]{:S(2)}) %copy-start) | copy-done | bytes 1572888
  83.2 3.8 %collective-permute-start.14 = (bf16[256,1024]{1,0:T(8,128)(2,1)}, bf16[256,1024]{1,0:T(8,128)(2,1)}, u32[]{:S(2)}, u32[]{:S(2)}) collective-permute-start(bf16[256,1024]{1,0:T(8,128)(2,1)} %get-tuple-element.49), channel_id=1, source_target_pairs={{0,1},{1,0},{2,3},{3,2},{4,5},{5,4},{6,7},{7,6},{8,9},{9,8},{10,11... | collective-permute-start | bytes 1572872 | tf_op jit(solution)/shard_map/ppermute | solution.py:23
  87.0 0.0 copy-start.1
  87.0 1.4 %copy-done.1 = bf16[768,1024]{1,0:T(8,128)(2,1)S(1)} copy-done((bf16[768,1024]{1,0:T(8,128)(2,1)S(1)}, bf16[768,1024]{1,0:T(8,128)(2,1)}, u32[]{:S(2)}) %copy-start.1) | copy-done | bytes 1572888
  88.4 3.6 %shard_map.65 = f32[256,1024]{1,0:T(8,128)S(1)} custom-call(s32[1]{0:T(128)} %bitcast.1.basis_ref, bf16[3840,8192]{1,0:T(8,128)(2,1)} %virt_ref.21, bf16[768,1024]{1,0:T(8,128)(2,1)S(1)} %copy-done.1, bf16[64,3840]{1,0:T(8,128)(2,1)S(1)} %get-tuple-element.29.refs_0_, bf16[64,3840]{1,0:T(8,128)(2,1)S(1)} %collective-permute-done.2.refs_1_, ...), custom_call_target="tpu_custom_call" | custom-call | flops 2013265920 | bytes 7864320 | tf_op jit(solution)/shard_map/pallas_call | solution.py:181
  92.0 0.0 collective-permute-done.12
  92.0 1.3 %convert_add_fusion.total_ref = f32[256,1024]{1,0:T(8,128)S(1)} fusion(bf16[256,1024]{1,0:T(8,128)(2,1)} %collective-permute-done.12, f32[256,1024]{1,0:T(8,128)S(1)} %shard_map.65, bf16[256,1024]{1,0:T(8,128)(2,1)S(1)} %collective-permute-done.10.refs_6_), kind=kLoop, calls=%fused_computation | loop fusion | flops 1048576 | bytes 3145728 | tf_op jit(solution)/shard_map/add | solution.py:293
  93.3 0.0 collective-permute-done.13.refs_1_
  93.3 1.2 %collective-permute-done.14.refs_0_ = bf16[256,1024]{1,0:T(8,128)(2,1)} collective-permute-done((bf16[256,1024]{1,0:T(8,128)(2,1)}, bf16[256,1024]{1,0:T(8,128)(2,1)}, u32[]{:S(2)}, u32[]{:S(2)}) %collective-permute-start.14) | collective-permute-done | bytes 524320 | tf_op jit(solution)/shard_map/ppermute | solution.py:23
  94.4 2.3 %shard_map.66 = bf16[1024,256]{1,0:T(8,128)(2,1)} custom-call(s32[1]{0:T(128)} %bitcast.aux_ref, f32[256,1024]{1,0:T(8,128)S(1)} %convert_add_fusion.total_ref, bf16[256,1024]{1,0:T(8,128)(2,1)} %collective-permute-done.14.refs_0_, bf16[256,1024]{1,0:T(8,128)(2,1)S(1)} %collective-permute-done.13.refs_1_), custom_call_target="tpu_custom_call" | custom-call | tf_op jit(solution)/shard_map/pallas_call | solution.py:215
Async XLA Ops:
  0.7 8.3 %collective-permute-start.1 = (bf16[8,1024]{1,0:T(8,128)(2,1)S(1)}, bf16[8,1024]{1,0:T(8,128)(2,1)S(1)}, u32[]{:S(2)}, u32[]{:S(2)}) collective-permute-start(bf16[8,1024]{1,0:T(8,128)(2,1)S(1)} %get-tuple-element.51), channel_id=1, source_target_pairs={{0,7},{1,2},{2,1},{3,4},{4,3},{5,6},{6,5},{7,0},{8,15},{9,10},{10,... | collective-permute-start | bytes 49160 | tf_op jit(solution)/shard_map/ppermute | solution.py:237
  6.7 3.7 %collective-permute-start = (bf16[8,1024]{1,0:T(8,128)(2,1)S(1)}, bf16[8,1024]{1,0:T(8,128)(2,1)S(1)}, u32[]{:S(2)}, u32[]{:S(2)}) collective-permute-start(bf16[8,1024]{1,0:T(8,128)(2,1)S(1)} %get-tuple-element.52), channel_id=1, source_target_pairs={{0,1},{1,0},{2,3},{3,2},{4,5},{5,4},{6,7},{7,6},{8,9},{9,8},{10,11... | collective-permute-start | bytes 49160 | tf_op jit(solution)/shard_map/ppermute | solution.py:23
  17.5 1.9 %collective-permute-start.2 = (bf16[64,3840]{1,0:T(8,128)(2,1)S(1)}, bf16[64,3840]{1,0:T(8,128)(2,1)S(1)}, u32[]{:S(2)}, u32[]{:S(2)}) collective-permute-start(bf16[64,3840]{1,0:T(8,128)(2,1)S(1)} %get-tuple-element.29.refs_0_), channel_id=1, source_target_pairs={{0,8},{8,0},{16,24},{24,16},{1,9},{9,1},{17,25},{25,17},{2,10},{10... | collective-permute-start | bytes 1474568 | tf_op jit(solution)/shard_map/ppermute | solution.py:23
  17.6 13.6 %collective-permute-start.3 = (bf16[64,3840]{1,0:T(8,128)(2,1)S(1)}, bf16[64,3840]{1,0:T(8,128)(2,1)S(1)}, u32[]{:S(2)}, u32[]{:S(2)}) collective-permute-start(bf16[64,3840]{1,0:T(8,128)(2,1)S(1)} %get-tuple-element.29.refs_0_), channel_id=1, source_target_pairs={{0,16},{8,24},{16,0},{24,8},{1,17},{9,25},{17,1},{25,9},{2,18},{10... | collective-permute-start | bytes 1474568 | tf_op jit(solution)/shard_map/ppermute | solution.py:23
  22.9 8.4 %collective-permute-start.4 = (bf16[128,1024]{1,0:T(8,128)(2,1)S(1)}, bf16[128,1024]{1,0:T(8,128)(2,1)S(1)}, u32[]{:S(2)}, u32[]{:S(2)}) collective-permute-start(bf16[128,1024]{1,0:T(8,128)(2,1)S(1)} %get-tuple-element.32), channel_id=1, source_target_pairs={{0,1},{1,0},{2,3},{3,2},{4,5},{5,4},{6,7},{7,6},{8,9},{9,8},{10,11... | collective-permute-start | bytes 786440 | tf_op jit(solution)/shard_map/ppermute | solution.py:23
  31.3 1.9 %collective-permute-start.5 = (bf16[64,3840]{1,0:T(8,128)(2,1)S(1)}, bf16[64,3840]{1,0:T(8,128)(2,1)S(1)}, u32[]{:S(2)}, u32[]{:S(2)}) collective-permute-start(bf16[64,3840]{1,0:T(8,128)(2,1)S(1)} %collective-permute-done.3.refs_0_.refs_2_), channel_id=1, source_target_pairs={{0,8},{8,0},{16,24},{24,16},{1,9},{9,1},{17,25},{25,17},{2,10},{10... | collective-permute-start | bytes 1474568 | tf_op jit(solution)/shard_map/ppermute | solution.py:23
  31.3 9.1 %collective-permute-start.6 = (bf16[128,1024]{1,0:T(8,128)(2,1)S(1)}, bf16[128,1024]{1,0:T(8,128)(2,1)S(1)}, u32[]{:S(2)}, u32[]{:S(2)}) collective-permute-start(bf16[128,1024]{1,0:T(8,128)(2,1)S(1)} %get-tuple-element.35), channel_id=1, source_target_pairs={{0,1},{1,0},{2,3},{3,2},{4,5},{5,4},{6,7},{7,6},{8,9},{9,8},{10,11... | collective-permute-start | bytes 786440 | tf_op jit(solution)/shard_map/ppermute | solution.py:23
  36.5 9.1 %collective-permute-start.7 = (bf16[128,1024]{1,0:T(8,128)(2,1)S(1)}, bf16[128,1024]{1,0:T(8,128)(2,1)S(1)}, u32[]{:S(2)}, u32[]{:S(2)}) collective-permute-start(bf16[128,1024]{1,0:T(8,128)(2,1)S(1)} %get-tuple-element.37), channel_id=1, source_target_pairs={{0,1},{1,0},{2,3},{3,2},{4,5},{5,4},{6,7},{7,6},{8,9},{9,8},{10,11... | collective-permute-start | bytes 786440 | tf_op jit(solution)/shard_map/ppermute | solution.py:23
  44.2 13.4 %collective-permute-start.8 = (bf16[256,1024]{1,0:T(8,128)(2,1)S(1)}, bf16[256,1024]{1,0:T(8,128)(2,1)S(1)}, u32[]{:S(2)}, u32[]{:S(2)}) collective-permute-start(bf16[256,1024]{1,0:T(8,128)(2,1)S(1)} %get-tuple-element.40), channel_id=1, source_target_pairs={{0,1},{1,0},{2,3},{3,2},{4,5},{5,4},{6,7},{7,6},{8,9},{9,8},{10,11... | collective-permute-start | bytes 1572872 | tf_op jit(solution)/shard_map/ppermute | solution.py:23
  49.2 13.8 %collective-permute-start.11 = (bf16[256,1024]{1,0:T(8,128)(2,1)S(1)}, bf16[256,1024]{1,0:T(8,128)(2,1)S(1)}, u32[]{:S(2)}, u32[]{:S(2)}) collective-permute-start(bf16[256,1024]{1,0:T(8,128)(2,1)S(1)} %get-tuple-element.43), channel_id=1, source_target_pairs={{0,2},{1,3},{6,4},{7,5},{8,10},{9,11},{14,12},{15,13},{16,18},{17,... | collective-permute-start | bytes 1572872 | tf_op jit(solution)/shard_map/ppermute | solution.py:284
  50.6 12.5 %collective-permute-start.10 = (bf16[256,1024]{1,0:T(8,128)(2,1)S(1)}, bf16[256,1024]{1,0:T(8,128)(2,1)S(1)}, u32[]{:S(2)}, u32[]{:S(2)}) collective-permute-start(bf16[256,1024]{1,0:T(8,128)(2,1)S(1)} %get-tuple-element.43), channel_id=1, source_target_pairs={{2,4},{3,5},{4,2},{5,3},{10,12},{11,13},{12,10},{13,11},{18,20},{1... | collective-permute-start | bytes 1572872 | tf_op jit(solution)/shard_map/ppermute | solution.py:283
  54.8 8.2 %collective-permute-start.9 = (bf16[128,1024]{1,0:T(8,128)(2,1)S(1)}, bf16[128,1024]{1,0:T(8,128)(2,1)S(1)}, u32[]{:S(2)}, u32[]{:S(2)}) collective-permute-start(bf16[128,1024]{1,0:T(8,128)(2,1)S(1)} %get-tuple-element.42), channel_id=1, source_target_pairs={{0,1},{1,0},{2,3},{3,2},{4,5},{5,4},{6,7},{7,6},{8,9},{9,8},{10,11... | collective-permute-start | bytes 786440 | tf_op jit(solution)/shard_map/ppermute | solution.py:23
  62.0 29.9 %collective-permute-start.12 = (bf16[256,1024]{1,0:T(8,128)(2,1)}, bf16[256,1024]{1,0:T(8,128)(2,1)}, u32[]{:S(2)}, u32[]{:S(2)}) collective-permute-start(bf16[256,1024]{1,0:T(8,128)(2,1)} %get-tuple-element.47), channel_id=1, source_target_pairs={{0,4},{1,5},{6,2},{7,3},{2,0},{3,1},{4,6},{5,7},{8,12},{9,13},{14,... | collective-permute-start | bytes 1572872 | tf_op jit(solution)/shard_map/ppermute | solution.py:287
  67.1 26.2 %collective-permute-start.13 = (bf16[256,1024]{1,0:T(8,128)(2,1)S(1)}, bf16[256,1024]{1,0:T(8,128)(2,1)S(1)}, u32[]{:S(2)}, u32[]{:S(2)}) collective-permute-start(bf16[256,1024]{1,0:T(8,128)(2,1)S(1)} %add_convert_fusion.refs_4_), channel_id=1, source_target_pairs={{2,6},{3,7},{4,0},{5,1},{0,2},{1,3},{6,4},{7,5},{10,14},{11,15},{1... | collective-permute-start | bytes 1572872 | tf_op jit(solution)/shard_map/ppermute | solution.py:290
  82.0 1.2 %copy-start = (bf16[768,1024]{1,0:T(8,128)(2,1)}, bf16[768,1024]{1,0:T(8,128)(2,1)S(1)}, u32[]{:S(2)}) copy-start(bf16[768,1024]{1,0:T(8,128)(2,1)S(1)} %get-tuple-element.46.first_ref) | copy-start | bytes 4718596
  83.2 11.3 %collective-permute-start.14 = (bf16[256,1024]{1,0:T(8,128)(2,1)}, bf16[256,1024]{1,0:T(8,128)(2,1)}, u32[]{:S(2)}, u32[]{:S(2)}) collective-permute-start(bf16[256,1024]{1,0:T(8,128)(2,1)} %get-tuple-element.49), channel_id=1, source_target_pairs={{0,1},{1,0},{2,3},{3,2},{4,5},{5,4},{6,7},{7,6},{8,9},{9,8},{10,11... | collective-permute-start | bytes 1572872 | tf_op jit(solution)/shard_map/ppermute | solution.py:23
  87.0 1.4 %copy-start.1 = (bf16[768,1024]{1,0:T(8,128)(2,1)S(1)}, bf16[768,1024]{1,0:T(8,128)(2,1)}, u32[]{:S(2)}) copy-start(bf16[768,1024]{1,0:T(8,128)(2,1)} %copy-done) | copy-start | bytes 4718596
